TPU v7x, 128 devices: a whole 4x4x4 slice. The times are simulated.
128 devices in a mesh: section: 8 (over x, y_lo), tile: 16 (over z, y_hi, core).
Axes of the slice: x: 4, y: 4 (y_hi: 2, y_lo: 2; y = y_hi * 2 + y_lo), z: 4, core: 2. Of those that a mesh axis runs over, the one named last changes fastest.
Arguments:
- latents: bfloat16 [8, 6144, 1536], P('section', 'tile'), may hold values from -6 to 6
- query_key_value_weight: bfloat16 [8, 1536, 4608], P('section'), may hold values from -0.15625 to 0.15625
- output_weight_stack: bfloat16 [8, 1536, 1536], P('section'), may hold values from -0.15625 to 0.15625
- layer_norm_gains: float32 [8, 1536], P('section'), may hold values from 0.5 to 2
- attended_tile_lists: int32 [16, 3], P('tile'), may hold values from 0 to 15, as said below
- neighbour_tile_count: int32 [16], P('tile'), may hold values from 1 to 3
Outputs:
- advanced: bfloat16 [8, 6144, 1536], P('section', 'tile')
Inputs may be any that keep to these rules, and one draw needn't show every extreme that they name: `attended_tile_lists`: the tiles listed for tile t lie among the tiles of the index of tile that holds t and of its two neighbours on that axis; the first entry is t itself and the first neighbour_tile_count[t] entries are distinct.
All inputs are finite; a program needn't handle non-finite values.
Results may differ from a plain program's by a relative error of at most 0.02.
Values may be sent and summed in bfloat16 or wider, within the bound.
No kernel may reach another device: no remote copies, remote signals or barrier semaphores. Data moves between devices by JAX's collectives and lax.ppermute only.
A program may use at most 128 MiB of HBM per device.

v0:
```python
import functools
import math

import jax
import jax.numpy as jnp
from jax import lax
from jax.experimental import pallas as pl
from jax.experimental.pallas import tpu as pltpu
from jax.sharding import PartitionSpec as P

HEADS = 12
HD = 128
D = 1536
TS = 384
HALF = TS // 2
THIRD = TS // 3
N_TILE = 16
N_SECTION = 8
PAIR = 2 * HD
PAIRS = HEADS // 2
SCALE = HD ** (-0.5) * math.log2(math.e)
OFF = -1e30
BOTH = ("section", "tile")
UNROLL = False
NEAR_VMEM = 14 * 2**20
FAR_VMEM = 14 * 2**20
NEAR_FLOPS = 0
FAR_FLOPS = 0


def normalize(hidden, gain):
    widened = hidden.astype(jnp.float32)
    square = jnp.mean(widened * widened, axis=-1, keepdims=True)
    return (widened * lax.rsqrt(square + 1e-06) * gain).astype(jnp.bfloat16)


def dot(a, b):
    return jnp.dot(a, b, preferred_element_type=jnp.float32)


def dot_t(a, b):
    return lax.dot_general(a, b, (((1,), (1,)), ((), ())), preferred_element_type=jnp.float32)


def columns(j, first=0):
    return pl.ds(pl.multiple_of(first + j * PAIR, PAIR), PAIR)


def near_kernel(which, count, flag_ref, own_ref, *refs):
    near_refs, (gain_ref, w_ref, _, q_ref, o_ref, lse_ref, normed, kept_k, kept_v) = refs[:count], refs[count:]
    normed[:TS, :] = normalize(own_ref[...], gain_ref[...])
    rows = TS // count
    for i, ref in enumerate(near_refs):
        normed[TS + i * rows : TS + (i + 1) * rows, :] = normalize(ref[...], gain_ref[...])
    bias = jnp.where(flag_ref[which] > 0, 0.0, OFF)
    lane = lax.broadcasted_iota(jnp.int32, lse_ref.shape, 1)
    lse_ref[...] = jnp.zeros_like(lse_ref)
    for head in range(2):
        kept_v[:, :, head * PAIR + HD : (head + 1) * PAIR] = jnp.ones((2, 2 * TS, HD), jnp.bfloat16)

    def project_q(j):
        q_ref[:, columns(j)] = (dot(normed[:TS, :], w_ref[:, columns(j)]) * SCALE).astype(jnp.bfloat16)

    def project_k(j, slot):
        kept_k[slot] = dot(normed[...], w_ref[:, columns(j, D)]).astype(jnp.bfloat16)

    def project_v(j, slot):
        v = dot(normed[...], w_ref[:, columns(j, 2 * D)]).astype(jnp.bfloat16)
        kept_v[slot, :, :HD] = v[:, :HD]
        kept_v[slot, :, PAIR : PAIR + HD] = v[:, HD:]

    def score(q, k, i):
        return dot_t(q[:, i * HD : (i + 1) * HD], k[:, i * HD : (i + 1) * HD])

    def weigh(s):
        s0, s1 = s[:, :TS], s[:, TS:]
        m = jnp.maximum(jnp.max(s0, axis=1, keepdims=True), jnp.max(s1, axis=1, keepdims=True) + bias)
        p0 = jnp.exp2(s0 - m).astype(jnp.bfloat16)
        p1 = jnp.exp2(s1 - (m - bias)).astype(jnp.bfloat16)
        return jnp.concatenate([p0, p1], axis=1), m

    def collect(p, m, v, j, i):
        mixed = dot(p, v[:, i * PAIR : (i + 1) * PAIR])
        total = mixed[:, HD:]
        first = pl.multiple_of(j * PAIR, PAIR) + i * HD
        o_ref[:, pl.ds(first, HD)] = mixed[:, :HD] / total
        lse_ref[...] = jnp.where(lane == 2 * j + i, m + jnp.log2(total), lse_ref[...])

    project_q(0)
    project_k(0, 0)
    project_v(0, 0)

    def step(j, more):
        slot = j % 2
        q, k, v = q_ref[:, columns(j)], kept_k[slot], kept_v[slot]
        s0 = score(q, k, 0)
        if more:
            project_q(j + 1)
        p0, m0 = weigh(s0)
        s1 = score(q, k, 1)
        if more:
            project_k(j + 1, 1 - slot)
        p1, m1 = weigh(s1)
        collect(p0, m0, v, j, 0)
        if more:
            project_v(j + 1, 1 - slot)
        collect(p1, m1, v, j, 1)

    steps(step)


def steps(step):
    if UNROLL:
        for j in range(PAIRS - 1):
            step(j, True)
    else:
        lax.fori_loop(0, PAIRS - 1, lambda j, carry: step(j, True) or carry, 0)
    step(PAIRS - 1, False)


def far_kernel(which, count, flag_ref, own_ref, *refs):
    far_refs, refs = refs[:count], refs[count:]
    gain_ref, q_ref, o_ref, lse_ref, w_ref, wo_ref, out_ref, normed, mixed, kept_k, kept_v = refs
    rows = TS // count
    for i, ref in enumerate(far_refs):
        normed[i * rows : (i + 1) * rows, :] = normalize(ref[...], gain_ref[...])
    bias = jnp.where(flag_ref[which] > 0, 0.0, OFF)
    lane = lax.broadcasted_iota(jnp.int32, lse_ref.shape, 1)
    for head in range(2):
        kept_v[:, :, head * PAIR + HD : (head + 1) * PAIR] = jnp.ones((2, TS, HD), jnp.bfloat16)

    def project_k(j, slot):
        kept_k[slot] = dot(normed[...], w_ref[:, columns(j, D)]).astype(jnp.bfloat16)

    def project_v(j, slot):
        v = dot(normed[...], w_ref[:, columns(j, 2 * D)]).astype(jnp.bfloat16)
        kept_v[slot, :, :HD] = v[:, :HD]
        kept_v[slot, :, PAIR : PAIR + HD] = v[:, HD:]

    def score(q, k, i):
        return dot_t(q[:, i * HD : (i + 1) * HD], k[:, i * HD : (i + 1) * HD])

    def weigh(s):
        m = jnp.max(s, axis=1, keepdims=True)
        return jnp.exp2(s - m).astype(jnp.bfloat16), m + bias

    def collect(p, m, v, j, i):
        both = dot(p, v[:, i * PAIR : (i + 1) * PAIR])
        before = jnp.sum(jnp.where(lane == 2 * j + i, lse_ref[...], 0.0), axis=1, keepdims=True)
        top = jnp.maximum(before, m)
        w0, w1 = jnp.exp2(before - top), jnp.exp2(m - top)
        first = pl.multiple_of(j * PAIR, PAIR) + i * HD
        o = (o_ref[:, pl.ds(first, HD)] * w0 + both[:, :HD] * w1) / (w0 + both[:, HD:] * w1)
        mixed[:, pl.ds(first, HD)] = o.astype(jnp.bfloat16)

    project_k(0, 0)
    project_v(0, 0)

    def step(j, more):
        slot = j % 2
        q, k, v = q_ref[:, columns(j)], kept_k[slot], kept_v[slot]
        s0 = score(q, k, 0)
        s1 = score(q, k, 1)
        p0, m0 = weigh(s0)
        if more:
            project_k(j + 1, 1 - slot)
        p1, m1 = weigh(s1)
        collect(p0, m0, v, j, 0)
        if more:
            project_v(j + 1, 1 - slot)
        collect(p1, m1, v, j, 1)

    steps(step)

    def finish(j, carry):
        update = dot(mixed[...], wo_ref[:, columns(j)])
        out_ref[:, columns(j)] = (own_ref[:, columns(j)].astype(jnp.float32) + update).astype(jnp.bfloat16)
        return carry

    lax.fori_loop(0, PAIRS, finish, 0, unroll=UNROLL)


SMEM = pl.BlockSpec(memory_space=pltpu.SMEM)
VMEM = pl.BlockSpec(memory_space=pltpu.VMEM)


def near_attention(which, flags, own, near, gain, wqkv, wo):
    return pl.pallas_call(
        functools.partial(near_kernel, which, len(near)),
        out_shape=(
            jax.ShapeDtypeStruct((TS, D), jnp.bfloat16),
            jax.ShapeDtypeStruct((TS, D), jnp.float32),
            jax.ShapeDtypeStruct((TS, HD), jnp.float32),
        ),
        in_specs=[SMEM] + [VMEM] * (4 + len(near)),
        out_specs=(VMEM, VMEM, VMEM),
        scratch_shapes=[
            pltpu.VMEM((2 * TS, D), jnp.bfloat16),
            pltpu.VMEM((2, 2 * TS, PAIR), jnp.bfloat16),
            pltpu.VMEM((2, 2 * TS, 2 * PAIR), jnp.bfloat16),
        ],
        compiler_params=pltpu.CompilerParams(vmem_limit_bytes=NEAR_VMEM),
        cost_estimate=pl.CostEstimate(flops=NEAR_FLOPS, bytes_accessed=0, transcendentals=0),
        name="near_attention",
    )(flags, own, *near, gain, wqkv, wo)


def far_attention(which, flags, own, far, gain, q, o, lse, wqkv, wo):
    return pl.pallas_call(
        functools.partial(far_kernel, which, len(far)),
        out_shape=jax.ShapeDtypeStruct((TS, D), jnp.bfloat16),
        in_specs=[SMEM] + [VMEM] * (7 + len(far)),
        out_specs=VMEM,
        scratch_shapes=[
            pltpu.VMEM((TS, D), jnp.bfloat16),
            pltpu.VMEM((TS, D), jnp.bfloat16),
            pltpu.VMEM((2, TS, PAIR), jnp.bfloat16),
            pltpu.VMEM((2, TS, 2 * PAIR), jnp.bfloat16),
        ],
        compiler_params=pltpu.CompilerParams(vmem_limit_bytes=FAR_VMEM),
        cost_estimate=pl.CostEstimate(flops=FAR_FLOPS, bytes_accessed=0, transcendentals=0),
        name="far_attention",
    )(flags, own, *far, gain, q, o, lse, wqkv, wo)


def place(t):
    z, r = divmod(t, 4)
    if r == 0:
        return 4 * ((z - 1) % 4) + 1
    if r == 3:
        return 4 * z
    return 4 * z + 1 + r


def other(t):
    return t + 1 if t % 2 else t - 1


def route(moves):
    return [(s * N_TILE + a, (s + step) % N_SECTION * N_TILE + b) for s in range(N_SECTION) for step, a, b in moves]


def step_out(s):
    return s + 1 if s % 2 == 0 else s - 1


TILES = range(N_TILE)
CORE_SWAP = route([(0, t, t ^ 1) for t in TILES])
NEXT_CHIP = route([(0, t, other(t)) for t in TILES if 0 <= other(t) < N_TILE])
FORWARD = route([(1, t, place(t)) for t in TILES])
PAIR_OUT = [(s * N_TILE + t, step_out(s) * N_TILE + place(t ^ 1)) for s in range(N_SECTION) for t in TILES]
PAIR_IN = [(step_out(s) * N_TILE + u, (s + 1) % N_SECTION * N_TILE + u) for s in range(N_SECTION) for u in TILES]
HOME = route([(1, place(t), t) for t in TILES])
SPREAD = [(t, place(t)) for t in TILES]


def pieces(block, rows):
    return [block[i : i + rows] for i in range(0, TS, rows)]


def on_device(latents, wqkv, wo, gains, lists, counts):
    own = latents[0]
    wqkv, wo = wqkv[0], wo[0]

    def send(perm, blocks):
        return [lax.ppermute(block, BOTH, perm) for block in blocks]

    far = send(NEXT_CHIP, [own])
    near = send(CORE_SWAP, [own])
    tile = lax.axis_index("tile")
    pair = tile ^ 1
    beyond = jnp.where(tile % 2 == 1, tile + 1, tile - 1)
    used = jnp.arange(lists.shape[1]) < counts[0]
    pair_used = jnp.any((lists[0] == pair) & used).astype(jnp.int32)
    beyond_used = jnp.any((lists[0] == beyond) & used).astype(jnp.int32)
    flags = jnp.stack([pair_used, beyond_used])

    q, o, lse = near_attention(0, flags, own, near, gains, wqkv, wo)
    flags, lse = lax.optimization_barrier((flags, lse))
    flags_next = lax.ppermute(flags, "tile", SPREAD)
    flags, flags_next = lax.optimization_barrier((flags, flags_next))
    own = far_attention(1, flags, own, far, gains, q, o, lse, wqkv, wo)
    far = send(PAIR_IN, send(PAIR_OUT, pieces(own, HALF)))
    (own,) = send(FORWARD, [own])
    near = send(CORE_SWAP, pieces(own, THIRD))
    q, o, lse = near_attention(1, flags_next, own, near, gains, wqkv, wo)
    own = far_attention(0, flags_next, own, far, gains, q, o, lse, wqkv, wo)
    (own,) = send(HOME, [own])
    return own[None]


def solution(mesh):
    return jax.shard_map(
        on_device,
        mesh=mesh,
        in_specs=(
            P("section", "tile", None),
            P("section", None, None),
            P("section", None, None),
            P("section", None),
            P("tile", None),
            P("tile"),
        ),
        out_specs=P("section", "tile", None),
        check_vma=False,
    )
```

profile of v0, /device:TPU:0, one launch (start us, length us, event | category | flops | bytes accessed | tf_op | source)
XLA Modules:
  0.0 146.5 jit_solution(4218604449692387825)
XLA Ops:
  0.0 0.7 collective-permute-start.2
  1.4 1.4 fusion.1
  2.8 1.3 add_convert_fusion.flag_ref
  4.1 5.0 %copy-done = bf16[1,1536,4608]{2,1,0:T(8,128)(2,1)S(1)} copy-done((bf16[1,1536,4608]{2,1,0:T(8,128)(2,1)S(1)}, bf16[1,1536,4608]{2,1,0:T(8,128)(2,1)}, u32[]{:S(2)}) %copy-start) | copy-done | bytes 14155800
  9.1 2.3 %copy-done.2 = bf16[1,1536,1536]{2,1,0:T(8,128)(2,1)S(1)} copy-done((bf16[1,1536,1536]{2,1,0:T(8,128)(2,1)S(1)}, bf16[1,1536,1536]{2,1,0:T(8,128)(2,1)}, u32[]{:S(2)}) %copy-start.2) | copy-done | bytes 4718616
  11.4 1.3 copy-done.4
  12.7 0.7 copy-done.5
  13.4 15.5 %near_attention.2 = (bf16[384,1536]{1,0:T(8,128)(2,1)S(1)}, f32[384,1536]{1,0:T(8,128)S(1)}, f32[384,128]{1,0:T(8,128)S(1)}) custom-call(s32[2]{0:T(128)S(1)} %add_convert_fusion.flag_ref, bf16[384,1536]{1,0:T(8,128)(2,1)S(1)} %bitcast.26, bf16[384,1536]{1,0:T(8,128)(2,1)S(1)} %collective-permute-done.refs_0_, f32[1,1536]{1,0:T(1,128)S(1)} %copy-done.5, ...), custom_call_target="tpu_custom_call" | custom-call | tf_op jit(solution)/shard_map/near_attention/pallas_call | solution.py:188
  29.0 8.3 %collective-permute-start.1 = (s32[2]{0:T(128)S(1)}, s32[2]{0:T(128)S(1)}, u32[]{:S(2)}, u32[]{:S(2)}) collective-permute-start(s32[2]{0:T(128)S(1)} %add_convert_fusion.flag_ref), channel_id=1, source_target_pairs={{0,13},{1,2},{2,3},{3,0},{4,1},{5,6},{6,7},{7,4},{8,5},{9,10},{10,... | collective-permute-start | bytes 32 | tf_op jit(solution)/shard_map/ppermute | solution.py:280
  37.2 1.3 collective-permute-done.1.flag_ref
  38.5 11.6 %far_attention.2 = bf16[384,1536]{1,0:T(8,128)(2,1)S(1)} custom-call(s32[2]{0:T(128)S(1)} %add_convert_fusion.flag_ref, bf16[384,1536]{1,0:T(8,128)(2,1)S(1)} %bitcast.27, bf16[384,1536]{1,0:T(8,128)(2,1)S(1)} %collective-permute-done.2.refs_0_, f32[1,1536]{1,0:T(1,128)S(1)} %copy-done.5, bf16[384,1536]{1,0:T(8,128)(2,1)S(1)} %get-tuple-element.19.refs_2_, ...), custom_call_target="tpu_custom_call" | custom-call | tf_op jit(solution)/shard_map/far_attention/pallas_call | solution.py:209
  50.1 3.1 %collective-permute-start.3 = (bf16[384,1536]{1,0:T(8,128)(2,1)S(1)}, bf16[384,1536]{1,0:T(8,128)(2,1)S(1)}, u32[]{:S(2)}, u32[]{:S(2)}) collective-permute-start(bf16[384,1536]{1,0:T(8,128)(2,1)S(1)} %far_attention.2), channel_id=1, source_target_pairs={{0,29},{1,18},{2,19},{3,16},{4,17},{5,22},{6,23},{7,20},{8,21},{9,... | collective-permute-start | bytes 3538952 | tf_op jit(solution)/shard_map/ppermute | solution.py:266
  53.4 3.2 %collective-permute-start.4 = (bf16[192,1536]{1,0:T(8,128)(2,1)S(1)}, bf16[192,1536]{1,0:T(8,128)(2,1)S(1)}, u32[]{:S(2)}, u32[]{:S(2)}) collective-permute-start(bf16[192,1536]{1,0:T(8,128)(2,1)S(1)} %get-tuple-element.31), channel_id=1, source_target_pairs={{0,18},{1,29},{2,16},{3,19},{4,22},{5,17},{6,20},{7,23},{8,26},{9,... | collective-permute-start | bytes 1769480 | tf_op jit(solution)/shard_map/ppermute | solution.py:266
  56.6 14.2 %collective-permute-done.6 = bf16[192,1536]{1,0:T(8,128)(2,1)S(1)} collective-permute-done((bf16[192,1536]{1,0:T(8,128)(2,1)S(1)}, bf16[192,1536]{1,0:T(8,128)(2,1)S(1)}, u32[]{:S(2)}, u32[]{:S(2)}) %collective-permute-start.6) | collective-permute-done | bytes 589856 | tf_op jit(solution)/shard_map/ppermute | solution.py:266
  70.8 3.4 %collective-permute-start.7 = (bf16[192,1536]{1,0:T(8,128)(2,1)S(1)}, bf16[192,1536]{1,0:T(8,128)(2,1)S(1)}, u32[]{:S(2)}, u32[]{:S(2)}) collective-permute-start(bf16[192,1536]{1,0:T(8,128)(2,1)S(1)} %collective-permute-done.6), channel_id=1, source_target_pairs={{16,16},{17,17},{18,18},{19,19},{20,20},{21,21},{22,22},{23,23},{2... | collective-permute-start | bytes 1769480 | tf_op jit(solution)/shard_map/ppermute | solution.py:266
  74.2 8.5 %collective-permute-done.4 = bf16[192,1536]{1,0:T(8,128)(2,1)S(1)} collective-permute-done((bf16[192,1536]{1,0:T(8,128)(2,1)S(1)}, bf16[192,1536]{1,0:T(8,128)(2,1)S(1)}, u32[]{:S(2)}, u32[]{:S(2)}) %collective-permute-start.4) | collective-permute-done | bytes 589856 | tf_op jit(solution)/shard_map/ppermute | solution.py:266
  82.7 2.8 %collective-permute-start.5 = (bf16[192,1536]{1,0:T(8,128)(2,1)S(1)}, bf16[192,1536]{1,0:T(8,128)(2,1)S(1)}, u32[]{:S(2)}, u32[]{:S(2)}) collective-permute-start(bf16[192,1536]{1,0:T(8,128)(2,1)S(1)} %collective-permute-done.4), channel_id=1, source_target_pairs={{16,16},{17,17},{18,18},{19,19},{20,20},{21,21},{22,22},{23,23},{2... | collective-permute-start | bytes 1769480 | tf_op jit(solution)/shard_map/ppermute | solution.py:266
  86.2 1.1 collective-permute-done.10.refs_2_
  87.4 0.6 collective-permute-done.9.refs_1_
  87.9 0.6 collective-permute-done.8.refs_0_
  88.5 15.6 %near_attention.3 = (bf16[384,1536]{1,0:T(8,128)(2,1)S(1)}, f32[384,1536]{1,0:T(8,128)S(1)}, f32[384,128]{1,0:T(8,128)S(1)}) custom-call(s32[2]{0:T(128)S(1)} %collective-permute-done.1.flag_ref, bf16[384,1536]{1,0:T(8,128)(2,1)S(1)} %collective-permute-done.3.own_ref, bf16[128,1536]{1,0:T(8,128)(2,1)S(1)} %collective-permute-done.8.refs_0_, ...), custom_call_target="tpu_custom_call" | custom-call | tf_op jit(solution)/shard_map/near_attention/pallas_call | solution.py:188
  104.1 11.5 %far_attention.3 = bf16[384,1536]{1,0:T(8,128)(2,1)S(1)} custom-call(s32[2]{0:T(128)S(1)} %collective-permute-done.1.flag_ref, bf16[384,1536]{1,0:T(8,128)(2,1)S(1)} %collective-permute-done.3.own_ref, bf16[192,1536]{1,0:T(8,128)(2,1)S(1)} %collective-permute-done.5.refs_0_, bf16[192,1536]{1,0:T(8,128)(2,1)S(1)} %collective-permute-done.7.refs_1_, ...), custom_call_target="tpu_custom_call" | custom-call | tf_op jit(solution)/shard_map/far_attention/pallas_call | solution.py:209
  115.7 29.8 %collective-permute-done.11 = bf16[384,1536]{1,0:T(8,128)(2,1)S(1)} collective-permute-done((bf16[384,1536]{1,0:T(8,128)(2,1)S(1)}, bf16[384,1536]{1,0:T(8,128)(2,1)S(1)}, u32[]{:S(2)}, u32[]{:S(2)}) %collective-permute-start.11) | collective-permute-done | bytes 1179680 | tf_op jit(solution)/shard_map/ppermute | solution.py:266
  145.5 1.0 copy.9
  (21 shorter events, 1.0 us)
Async XLA Ops:
  0.0 4.1 %collective-permute-start = (bf16[384,1536]{1,0:T(8,128)(2,1)}, bf16[384,1536]{1,0:T(8,128)(2,1)S(1)}, u32[]{:S(2)}, u32[]{:S(2)}) collective-permute-start(bf16[384,1536]{1,0:T(8,128)(2,1)} %bitcast.24), channel_id=1, source_target_pairs={{0,1},{1,0},{2,3},{3,2},{4,5},{5,4},{6,7},{7,6},{8,9},{9,8},{10,11... | collective-permute-start | bytes 3538952 | tf_op jit(solution)/shard_map/ppermute | solution.py:266
  0.0 38.5 %collective-permute-start.2 = (bf16[384,1536]{1,0:T(8,128)(2,1)}, bf16[384,1536]{1,0:T(8,128)(2,1)S(1)}, u32[]{:S(2)}, u32[]{:S(2)}) collective-permute-start(bf16[384,1536]{1,0:T(8,128)(2,1)} %bitcast.25), channel_id=1, source_target_pairs={{1,2},{2,1},{3,4},{4,3},{5,6},{6,5},{7,8},{8,7},{9,10},{10,9},{11,... | collective-permute-start | bytes 3538952 | tf_op jit(solution)/shard_map/ppermute | solution.py:266
  4.1 5.0 %copy-start = (bf16[1,1536,4608]{2,1,0:T(8,128)(2,1)S(1)}, bf16[1,1536,4608]{2,1,0:T(8,128)(2,1)}, u32[]{:S(2)}) copy-start(bf16[1,1536,4608]{2,1,0:T(8,128)(2,1)} %param.7) | copy-start | bytes 42467332
  9.1 2.3 %copy-start.2 = (bf16[1,1536,1536]{2,1,0:T(8,128)(2,1)S(1)}, bf16[1,1536,1536]{2,1,0:T(8,128)(2,1)}, u32[]{:S(2)}) copy-start(bf16[1,1536,1536]{2,1,0:T(8,128)(2,1)} %param.8) | copy-start | bytes 14155780
  11.4 1.3 copy-start.4
  12.7 0.7 copy-start.5
  13.4 25.1 %copy-start.1 = (bf16[1,1536,4608]{2,1,0:T(8,128)(2,1)S(1)}, bf16[1,1536,4608]{2,1,0:T(8,128)(2,1)}, u32[]{:S(2)}) copy-start(bf16[1,1536,4608]{2,1,0:T(8,128)(2,1)} %param.7) | copy-start | bytes 42467332
  13.4 25.1 %copy-start.3 = (bf16[1,1536,1536]{2,1,0:T(8,128)(2,1)S(1)}, bf16[1,1536,1536]{2,1,0:T(8,128)(2,1)}, u32[]{:S(2)}) copy-start(bf16[1,1536,1536]{2,1,0:T(8,128)(2,1)} %param.8) | copy-start | bytes 14155780
  29.0 9.6 %collective-permute-start.1 = (s32[2]{0:T(128)S(1)}, s32[2]{0:T(128)S(1)}, u32[]{:S(2)}, u32[]{:S(2)}) collective-permute-start(s32[2]{0:T(128)S(1)} %add_convert_fusion.flag_ref), channel_id=1, source_target_pairs={{0,13},{1,2},{2,3},{3,0},{4,1},{5,6},{6,7},{7,4},{8,5},{9,10},{10,... | collective-permute-start | bytes 32 | tf_op jit(solution)/shard_map/ppermute | solution.py:280
  50.1 35.3 %collective-permute-start.3 = (bf16[384,1536]{1,0:T(8,128)(2,1)S(1)}, bf16[384,1536]{1,0:T(8,128)(2,1)S(1)}, u32[]{:S(2)}, u32[]{:S(2)}) collective-permute-start(bf16[384,1536]{1,0:T(8,128)(2,1)S(1)} %far_attention.2), channel_id=1, source_target_pairs={{0,29},{1,18},{2,19},{3,16},{4,17},{5,22},{6,23},{7,20},{8,21},{9,... | collective-permute-start | bytes 3538952 | tf_op jit(solution)/shard_map/ppermute | solution.py:266
  53.3 17.5 %collective-permute-start.6 = (bf16[192,1536]{1,0:T(8,128)(2,1)S(1)}, bf16[192,1536]{1,0:T(8,128)(2,1)S(1)}, u32[]{:S(2)}, u32[]{:S(2)}) collective-permute-start(bf16[192,1536]{1,0:T(8,128)(2,1)S(1)} %get-tuple-element.30), channel_id=1, source_target_pairs={{0,18},{1,29},{2,16},{3,19},{4,22},{5,17},{6,20},{7,23},{8,26},{9,... | collective-permute-start | bytes 1769480 | tf_op jit(solution)/shard_map/ppermute | solution.py:266
  53.4 29.2 %collective-permute-start.4 = (bf16[192,1536]{1,0:T(8,128)(2,1)S(1)}, bf16[192,1536]{1,0:T(8,128)(2,1)S(1)}, u32[]{:S(2)}, u32[]{:S(2)}) collective-permute-start(bf16[192,1536]{1,0:T(8,128)(2,1)S(1)} %get-tuple-element.31), channel_id=1, source_target_pairs={{0,18},{1,29},{2,16},{3,19},{4,22},{5,17},{6,20},{7,23},{8,26},{9,... | collective-permute-start | bytes 1769480 | tf_op jit(solution)/shard_map/ppermute | solution.py:266
  70.8 33.2 %collective-permute-start.7 = (bf16[192,1536]{1,0:T(8,128)(2,1)S(1)}, bf16[192,1536]{1,0:T(8,128)(2,1)S(1)}, u32[]{:S(2)}, u32[]{:S(2)}) collective-permute-start(bf16[192,1536]{1,0:T(8,128)(2,1)S(1)} %collective-permute-done.6), channel_id=1, source_target_pairs={{16,16},{17,17},{18,18},{19,19},{20,20},{21,21},{22,22},{23,23},{2... | collective-permute-start | bytes 1769480 | tf_op jit(solution)/shard_map/ppermute | solution.py:266
  82.7 21.4 %collective-permute-start.5 = (bf16[192,1536]{1,0:T(8,128)(2,1)S(1)}, bf16[192,1536]{1,0:T(8,128)(2,1)S(1)}, u32[]{:S(2)}, u32[]{:S(2)}) collective-permute-start(bf16[192,1536]{1,0:T(8,128)(2,1)S(1)} %collective-permute-done.4), channel_id=1, source_target_pairs={{16,16},{17,17},{18,18},{19,19},{20,20},{21,21},{22,22},{23,23},{2... | collective-permute-start | bytes 1769480 | tf_op jit(solution)/shard_map/ppermute | solution.py:266
  85.6 1.8 %collective-permute-start.10 = (bf16[128,1536]{1,0:T(8,128)(2,1)S(1)}, bf16[128,1536]{1,0:T(8,128)(2,1)S(1)}, u32[]{:S(2)}, u32[]{:S(2)}) collective-permute-start(bf16[128,1536]{1,0:T(8,128)(2,1)S(1)} %get-tuple-element.27), channel_id=1, source_target_pairs={{0,1},{1,0},{2,3},{3,2},{4,5},{5,4},{6,7},{7,6},{8,9},{9,8},{10,11... | collective-permute-start | bytes 1179656 | tf_op jit(solution)/shard_map/ppermute | solution.py:266
  85.6 2.3 %collective-permute-start.9 = (bf16[128,1536]{1,0:T(8,128)(2,1)S(1)}, bf16[128,1536]{1,0:T(8,128)(2,1)S(1)}, u32[]{:S(2)}, u32[]{:S(2)}) collective-permute-start(bf16[128,1536]{1,0:T(8,128)(2,1)S(1)} %get-tuple-element.28), channel_id=1, source_target_pairs={{0,1},{1,0},{2,3},{3,2},{4,5},{5,4},{6,7},{7,6},{8,9},{9,8},{10,11... | collective-permute-start | bytes 1179656 | tf_op jit(solution)/shard_map/ppermute | solution.py:266
  86.1 2.3 %collective-permute-start.8 = (bf16[128,1536]{1,0:T(8,128)(2,1)S(1)}, bf16[128,1536]{1,0:T(8,128)(2,1)S(1)}, u32[]{:S(2)}, u32[]{:S(2)}) collective-permute-start(bf16[128,1536]{1,0:T(8,128)(2,1)S(1)} %get-tuple-element.29), channel_id=1, source_target_pairs={{0,1},{1,0},{2,3},{3,2},{4,5},{5,4},{6,7},{7,6},{8,9},{9,8},{10,11... | collective-permute-start | bytes 1179656 | tf_op jit(solution)/shard_map/ppermute | solution.py:266
  115.6 29.9 %collective-permute-start.11 = (bf16[384,1536]{1,0:T(8,128)(2,1)S(1)}, bf16[384,1536]{1,0:T(8,128)(2,1)S(1)}, u32[]{:S(2)}, u32[]{:S(2)}) collective-permute-start(bf16[384,1536]{1,0:T(8,128)(2,1)S(1)} %far_attention.3), channel_id=1, source_target_pairs={{13,16},{2,17},{3,18},{0,19},{1,20},{6,21},{7,22},{4,23},{5,24},{1... | collective-permute-start | bytes 3538952 | tf_op jit(solution)/shard_map/ppermute | solution.py:266
where the time goes:
time: 147 us
  waiting for transfers between devices  56 us (38%)
  Pallas kernels  54.2 us (37%)
  starting transfers between devices  22.3 us (15%)
  local copies, waits for them, and re-layouts  10.5 us (7%)
  other arithmetic  2.68 us (2%)
    ppermute x11, waiting for transfers between devices, send(): return [lax.ppermute(block, BOTH, perm) for block in blocks]  54.7 us
    pallas_call x2, Pallas kernels, near_attention(): pl.pallas_call(functools.partial(near_kernel, which, len(near)), out_shap...  31.1 us
    pallas_call x2, Pallas kernels, far_attention(): pl.pallas_call(functools.partial(far_kernel, which, len(far)), out_shape=...  23.1 us
    ppermute x11, starting transfers between devices, send(): return [lax.ppermute(block, BOTH, perm) for block in blocks]  14 us
    unnamed x13, local copies, waits for them, and re-layouts  10.3 us
    ppermute x1, starting transfers between devices, on_device(): flags_next = lax.ppermute(flags, 'tile', SPREAD)  8.28 us
  transfers between devices with their start and end apart: 12, of which 7 were waited for; matrix products, arithmetic and copies ran while one was open for 2% of the time, Pallas kernels for 21%

commit v1 on v0

--- a/solution.py
+++ b/solution.py
@@ -14,6 +14,7 @@
 TS = 384
 HALF = TS // 2
 THIRD = TS // 3
+WIDE = 512
 N_TILE = 16
 N_SECTION = 8
 PAIR = 2 * HD
@@ -46,13 +47,20 @@
     return pl.ds(pl.multiple_of(first + j * PAIR, PAIR), PAIR)
 
 
-def near_kernel(which, count, flag_ref, own_ref, *refs):
+def switch(on):
+    return jnp.where(on, 0.0, OFF)
+
+
+def near_kernel(count, flag_ref, own_ref, *refs):
     near_refs, (gain_ref, w_ref, _, q_ref, o_ref, lse_ref, normed, kept_k, kept_v) = refs[:count], refs[count:]
-    normed[:TS, :] = normalize(own_ref[...], gain_ref[...])
+    normed[:TS, :] = normalize(own_ref[:TS, :], gain_ref[...])
     rows = TS // count
     for i, ref in enumerate(near_refs):
         normed[TS + i * rows : TS + (i + 1) * rows, :] = normalize(ref[...], gain_ref[...])
-    bias = jnp.where(flag_ref[which] > 0, 0.0, OFF)
+    if own_ref.shape[0] > TS:
+        bias = switch(own_ref[TS : TS + 8, :HD].astype(jnp.float32) > 0)[:1, :1]
+    else:
+        bias = switch(flag_ref[0] > 0)
     lane = lax.broadcasted_iota(jnp.int32, lse_ref.shape, 1)
     lse_ref[...] = jnp.zeros_like(lse_ref)
     for head in range(2):
@@ -118,13 +126,18 @@
     step(PAIRS - 1, False)
 
 
-def far_kernel(which, count, flag_ref, own_ref, *refs):
+def far_kernel(count, flag_ref, own_ref, *refs):
     far_refs, refs = refs[:count], refs[count:]
     gain_ref, q_ref, o_ref, lse_ref, w_ref, wo_ref, out_ref, normed, mixed, kept_k, kept_v = refs
     rows = TS // count
     for i, ref in enumerate(far_refs):
         normed[i * rows : (i + 1) * rows, :] = normalize(ref[...], gain_ref[...])
-    bias = jnp.where(flag_ref[which] > 0, 0.0, OFF)
+    if own_ref.shape[0] > TS:
+        bias = switch(own_ref[TS + 8 :, :HD].astype(jnp.float32) > 0)[:1, :1]
+    else:
+        bias = switch(flag_ref[1] > 0)
+        out_ref[TS : TS + 8, :] = jnp.full((8, D), flag_ref[1], jnp.int32).astype(jnp.float32).astype(jnp.bfloat16)
+        out_ref[TS + 8 :, :] = jnp.full((8, D), flag_ref[0], jnp.int32).astype(jnp.float32).astype(jnp.bfloat16)
     lane = lax.broadcasted_iota(jnp.int32, lse_ref.shape, 1)
     for head in range(2):
         kept_v[:, :, head * PAIR + HD : (head + 1) * PAIR] = jnp.ones((2, TS, HD), jnp.bfloat16)
@@ -173,20 +186,21 @@
     steps(step)
 
     def finish(j, carry):
-        update = dot(mixed[...], wo_ref[:, columns(j)])
-        out_ref[:, columns(j)] = (own_ref[:, columns(j)].astype(jnp.float32) + update).astype(jnp.bfloat16)
+        cut = pl.ds(pl.multiple_of(j * WIDE, WIDE), WIDE)
+        update = dot(mixed[...], wo_ref[:, cut])
+        out_ref[:TS, cut] = (own_ref[:TS, cut].astype(jnp.float32) + update).astype(jnp.bfloat16)
         return carry
 
-    lax.fori_loop(0, PAIRS, finish, 0, unroll=UNROLL)
+    lax.fori_loop(0, D // WIDE, finish, 0)
 
 
 SMEM = pl.BlockSpec(memory_space=pltpu.SMEM)
 VMEM = pl.BlockSpec(memory_space=pltpu.VMEM)
 
 
-def near_attention(which, flags, own, near, gain, wqkv, wo):
+def near_attention(flags, own, near, gain, wqkv, wo):
     return pl.pallas_call(
-        functools.partial(near_kernel, which, len(near)),
+        functools.partial(near_kernel, len(near)),
         out_shape=(
             jax.ShapeDtypeStruct((TS, D), jnp.bfloat16),
             jax.ShapeDtypeStruct((TS, D), jnp.float32),
@@ -205,10 +219,10 @@
     )(flags, own, *near, gain, wqkv, wo)
 
 
-def far_attention(which, flags, own, far, gain, q, o, lse, wqkv, wo):
+def far_attention(rows, flags, own, far, gain, q, o, lse, wqkv, wo):
     return pl.pallas_call(
-        functools.partial(far_kernel, which, len(far)),
-        out_shape=jax.ShapeDtypeStruct((TS, D), jnp.bfloat16),
+        functools.partial(far_kernel, len(far)),
+        out_shape=jax.ShapeDtypeStruct((rows, D), jnp.bfloat16),
         in_specs=[SMEM] + [VMEM] * (7 + len(far)),
         out_specs=VMEM,
         scratch_shapes=[
@@ -251,7 +265,6 @@
 PAIR_OUT = [(s * N_TILE + t, step_out(s) * N_TILE + place(t ^ 1)) for s in range(N_SECTION) for t in TILES]
 PAIR_IN = [(step_out(s) * N_TILE + u, (s + 1) % N_SECTION * N_TILE + u) for s in range(N_SECTION) for u in TILES]
 HOME = route([(1, place(t), t) for t in TILES])
-SPREAD = [(t, place(t)) for t in TILES]
 
 
 def pieces(block, rows):
@@ -275,16 +288,13 @@
     beyond_used = jnp.any((lists[0] == beyond) & used).astype(jnp.int32)
     flags = jnp.stack([pair_used, beyond_used])
 
-    q, o, lse = near_attention(0, flags, own, near, gains, wqkv, wo)
-    flags, lse = lax.optimization_barrier((flags, lse))
-    flags_next = lax.ppermute(flags, "tile", SPREAD)
-    flags, flags_next = lax.optimization_barrier((flags, flags_next))
-    own = far_attention(1, flags, own, far, gains, q, o, lse, wqkv, wo)
+    q, o, lse = near_attention(flags, own, near, gains, wqkv, wo)
+    own = far_attention(TS + 16, flags, own, far, gains, q, o, lse, wqkv, wo)
     far = send(PAIR_IN, send(PAIR_OUT, pieces(own, HALF)))
     (own,) = send(FORWARD, [own])
     near = send(CORE_SWAP, pieces(own, THIRD))
-    q, o, lse = near_attention(1, flags_next, own, near, gains, wqkv, wo)
-    own = far_attention(0, flags_next, own, far, gains, q, o, lse, wqkv, wo)
+    q, o, lse = near_attention(flags, own, near, gains, wqkv, wo)
+    own = far_attention(TS, flags, own, far, gains, q, o, lse, wqkv, wo)
     (own,) = send(HOME, [own])
     return own[None]
 

time: 147 us -> 143 us (0.973)
  starting transfers between devices: 22.3 us -> 18.5 us
    ppermute x1 -> x0, starting transfers between devices: 8.28 us -> none  [on_device(): flags_next = lax.ppermute(flags, 'tile', SPREAD)]
    ppermute x11, starting transfers between devices: 14 us -> 18.5 us  [send(): return [lax.ppermute(block, BOTH, perm) for block in blocks]]
    unnamed x13 -> x15, local copies, waits for them, and re-layouts: 10.3 us -> 10.3 us
  transfers between devices with their start and end apart: 12 -> 11, of which waited for: 7 -> 6; matrix products, arithmetic and copies ran while one was open for 2% -> 2% of each run, Pallas kernels for 21% -> 22%
where the time goes in v1:
time: 143 us
  waiting for transfers between devices  56.2 us (39%)
  Pallas kernels  54 us (38%)
  starting transfers between devices  18.5 us (13%)
  local copies, waits for them, and re-layouts  10.5 us (7%)
  other arithmetic  2.68 us (2%)
    ppermute x11, waiting for transfers between devices, send(): return [lax.ppermute(block, BOTH, perm) for block in blocks]  56.2 us
    pallas_call x2, Pallas kernels, near_attention(): pl.pallas_call(functools.partial(near_kernel, len(near)), out_shape=(jax....  31.7 us
    pallas_call x2, Pallas kernels, far_attention(): pl.pallas_call(functools.partial(far_kernel, len(far)), out_shape=jax.Sha...  22.3 us
    ppermute x11, starting transfers between devices, send(): return [lax.ppermute(block, BOTH, perm) for block in blocks]  18.5 us
    unnamed x15, local copies, waits for them, and re-layouts  10.3 us
  transfers between devices with their start and end apart: 11, of which 6 were waited for; matrix products, arithmetic and copies ran while one was open for 2% of the time, Pallas kernels for 22%

profile of v1, /device:TPU:0, one launch (start us, length us, event | category | flops | bytes accessed | tf_op | source)
XLA Modules:
  0.0 142.7 jit_solution(3098018934126407819)
XLA Ops:
  0.0 0.7 collective-permute-start
  1.4 1.4 fusion.1
  2.8 1.3 add_convert_fusion.flag_ref
  4.1 5.0 %copy-done = bf16[1,1536,4608]{2,1,0:T(8,128)(2,1)S(1)} copy-done((bf16[1,1536,4608]{2,1,0:T(8,128)(2,1)S(1)}, bf16[1,1536,4608]{2,1,0:T(8,128)(2,1)}, u32[]{:S(2)}) %copy-start) | copy-done | bytes 14155800
  9.1 2.3 %copy-done.2 = bf16[1,1536,1536]{2,1,0:T(8,128)(2,1)S(1)} copy-done((bf16[1,1536,1536]{2,1,0:T(8,128)(2,1)S(1)}, bf16[1,1536,1536]{2,1,0:T(8,128)(2,1)}, u32[]{:S(2)}) %copy-start.2) | copy-done | bytes 4718616
  11.4 1.3 copy-done.4
  12.7 0.7 copy-done.5
  13.4 15.5 %near_attention.2 = (bf16[384,1536]{1,0:T(8,128)(2,1)S(1)}, f32[384,1536]{1,0:T(8,128)S(1)}, f32[384,128]{1,0:T(8,128)S(1)}) custom-call(s32[2]{0:T(128)S(1)} %add_convert_fusion.flag_ref, bf16[384,1536]{1,0:T(8,128)(2,1)S(1)} %bitcast.26, bf16[384,1536]{1,0:T(8,128)(2,1)S(1)} %collective-permute-done.1.refs_0_, f32[1,1536]{1,0:T(1,128)S(1)} %copy-done.5, ...), custom_call_target="tpu_custom_call" | custom-call | tf_op jit(solution)/shard_map/near_attention/pallas_call | solution.py:202
  29.0 11.1 %far_attention.2 = bf16[400,1536]{1,0:T(8,128)(2,1)S(1)} custom-call(s32[2]{0:T(128)S(1)} %add_convert_fusion.flag_ref, bf16[384,1536]{1,0:T(8,128)(2,1)S(1)} %bitcast.27, bf16[384,1536]{1,0:T(8,128)(2,1)S(1)} %collective-permute-done.refs_0_, f32[1,1536]{1,0:T(1,128)S(1)} %copy-done.5, bf16[384,1536]{1,0:T(8,128)(2,1)S(1)} %get-tuple-element.11.refs_2_, ...), custom_call_target="tpu_custom_call" | custom-call | tf_op jit(solution)/shard_map/far_attention/pallas_call | solution.py:223
  40.1 8.4 %collective-permute-start.2 = (bf16[400,1536]{1,0:T(8,128)(2,1)S(1)}, bf16[400,1536]{1,0:T(8,128)(2,1)S(1)}, u32[]{:S(2)}, u32[]{:S(2)}) collective-permute-start(bf16[400,1536]{1,0:T(8,128)(2,1)S(1)} %far_attention.2), channel_id=1, source_target_pairs={{0,29},{1,18},{2,19},{3,16},{4,17},{5,22},{6,23},{7,20},{8,21},{9,... | collective-permute-start | bytes 3686408 | tf_op jit(solution)/shard_map/ppermute | solution.py:279
  48.5 0.2 collective-permute-start.5
  48.7 3.2 %collective-permute-start.3 = (bf16[192,1536]{1,0:T(8,128)(2,1)S(1)}, bf16[192,1536]{1,0:T(8,128)(2,1)S(1)}, u32[]{:S(2)}, u32[]{:S(2)}) collective-permute-start(bf16[192,1536]{1,0:T(8,128)(2,1)S(1)} %get-tuple-element.23), channel_id=1, source_target_pairs={{0,18},{1,29},{2,16},{3,19},{4,22},{5,17},{6,20},{7,23},{8,26},{9,... | collective-permute-start | bytes 1769480 | tf_op jit(solution)/shard_map/ppermute | solution.py:279
  51.9 14.2 %collective-permute-done.5 = bf16[192,1536]{1,0:T(8,128)(2,1)S(1)} collective-permute-done((bf16[192,1536]{1,0:T(8,128)(2,1)S(1)}, bf16[192,1536]{1,0:T(8,128)(2,1)S(1)}, u32[]{:S(2)}, u32[]{:S(2)}) %collective-permute-start.5) | collective-permute-done | bytes 589856 | tf_op jit(solution)/shard_map/ppermute | solution.py:279
  66.0 3.4 %collective-permute-start.6 = (bf16[192,1536]{1,0:T(8,128)(2,1)S(1)}, bf16[192,1536]{1,0:T(8,128)(2,1)S(1)}, u32[]{:S(2)}, u32[]{:S(2)}) collective-permute-start(bf16[192,1536]{1,0:T(8,128)(2,1)S(1)} %collective-permute-done.5), channel_id=1, source_target_pairs={{16,16},{17,17},{18,18},{19,19},{20,20},{21,21},{22,22},{23,23},{2... | collective-permute-start | bytes 1769480 | tf_op jit(solution)/shard_map/ppermute | solution.py:279
  69.5 7.7 %collective-permute-done.3 = bf16[192,1536]{1,0:T(8,128)(2,1)S(1)} collective-permute-done((bf16[192,1536]{1,0:T(8,128)(2,1)S(1)}, bf16[192,1536]{1,0:T(8,128)(2,1)S(1)}, u32[]{:S(2)}, u32[]{:S(2)}) %collective-permute-start.3) | collective-permute-done | bytes 589856 | tf_op jit(solution)/shard_map/ppermute | solution.py:279
  77.2 1.9 %collective-permute-start.4 = (bf16[192,1536]{1,0:T(8,128)(2,1)S(1)}, bf16[192,1536]{1,0:T(8,128)(2,1)S(1)}, u32[]{:S(2)}, u32[]{:S(2)}) collective-permute-start(bf16[192,1536]{1,0:T(8,128)(2,1)S(1)} %collective-permute-done.3), channel_id=1, source_target_pairs={{16,16},{17,17},{18,18},{19,19},{20,20},{21,21},{22,22},{23,23},{2... | collective-permute-start | bytes 1769480 | tf_op jit(solution)/shard_map/ppermute | solution.py:279
  79.3 0.5 collective-permute-start.8
  79.9 1.1 collective-permute-done.9.refs_2_
  81.0 0.6 collective-permute-done.8.refs_1_
  81.6 0.6 collective-permute-done.7.refs_0_
  82.1 16.2 %near_attention.3 = (bf16[384,1536]{1,0:T(8,128)(2,1)S(1)}, f32[384,1536]{1,0:T(8,128)S(1)}, f32[384,128]{1,0:T(8,128)S(1)}) custom-call(s32[2]{0:T(128)S(1)} %add_convert_fusion.flag_ref, bf16[400,1536]{1,0:T(8,128)(2,1)S(1)} %collective-permute-done.2.own_ref, bf16[128,1536]{1,0:T(8,128)(2,1)S(1)} %collective-permute-done.7.refs_0_, ...), custom_call_target="tpu_custom_call" | custom-call | tf_op jit(solution)/shard_map/near_attention/pallas_call | solution.py:202
  98.4 11.2 %far_attention.3 = bf16[384,1536]{1,0:T(8,128)(2,1)S(1)} custom-call(s32[2]{0:T(128)S(1)} %add_convert_fusion.flag_ref, bf16[400,1536]{1,0:T(8,128)(2,1)S(1)} %collective-permute-done.2.own_ref, bf16[192,1536]{1,0:T(8,128)(2,1)S(1)} %collective-permute-done.4.refs_0_, bf16[192,1536]{1,0:T(8,128)(2,1)S(1)} %collective-permute-done.6.refs_1_, ...), custom_call_target="tpu_custom_call" | custom-call | tf_op jit(solution)/shard_map/far_attention/pallas_call | solution.py:223
  109.7 32.0 %collective-permute-done.10 = bf16[384,1536]{1,0:T(8,128)(2,1)S(1)} collective-permute-done((bf16[384,1536]{1,0:T(8,128)(2,1)S(1)}, bf16[384,1536]{1,0:T(8,128)(2,1)S(1)}, u32[]{:S(2)}, u32[]{:S(2)}) %collective-permute-start.10) | collective-permute-done | bytes 1179680 | tf_op jit(solution)/shard_map/ppermute | solution.py:279
  141.7 1.0 copy.9
  (21 shorter events, 0.4 us)
Async XLA Ops:
  0.0 4.1 %collective-permute-start.1 = (bf16[384,1536]{1,0:T(8,128)(2,1)}, bf16[384,1536]{1,0:T(8,128)(2,1)S(1)}, u32[]{:S(2)}, u32[]{:S(2)}) collective-permute-start(bf16[384,1536]{1,0:T(8,128)(2,1)} %bitcast.24), channel_id=1, source_target_pairs={{0,1},{1,0},{2,3},{3,2},{4,5},{5,4},{6,7},{7,6},{8,9},{9,8},{10,11... | collective-permute-start | bytes 3538952 | tf_op jit(solution)/shard_map/ppermute | solution.py:279
  0.0 29.0 %collective-permute-start = (bf16[384,1536]{1,0:T(8,128)(2,1)}, bf16[384,1536]{1,0:T(8,128)(2,1)S(1)}, u32[]{:S(2)}, u32[]{:S(2)}) collective-permute-start(bf16[384,1536]{1,0:T(8,128)(2,1)} %bitcast.25), channel_id=1, source_target_pairs={{1,2},{2,1},{3,4},{4,3},{5,6},{6,5},{7,8},{8,7},{9,10},{10,9},{11,... | collective-permute-start | bytes 3538952 | tf_op jit(solution)/shard_map/ppermute | solution.py:279
  4.1 5.0 %copy-start = (bf16[1,1536,4608]{2,1,0:T(8,128)(2,1)S(1)}, bf16[1,1536,4608]{2,1,0:T(8,128)(2,1)}, u32[]{:S(2)}) copy-start(bf16[1,1536,4608]{2,1,0:T(8,128)(2,1)} %param.7) | copy-start | bytes 42467332
  9.1 2.3 %copy-start.2 = (bf16[1,1536,1536]{2,1,0:T(8,128)(2,1)S(1)}, bf16[1,1536,1536]{2,1,0:T(8,128)(2,1)}, u32[]{:S(2)}) copy-start(bf16[1,1536,1536]{2,1,0:T(8,128)(2,1)} %param.8) | copy-start | bytes 14155780
  11.4 1.3 copy-start.4
  12.7 0.7 copy-start.5
  13.4 15.6 %copy-start.1 = (bf16[1,1536,4608]{2,1,0:T(8,128)(2,1)S(1)}, bf16[1,1536,4608]{2,1,0:T(8,128)(2,1)}, u32[]{:S(2)}) copy-start(bf16[1,1536,4608]{2,1,0:T(8,128)(2,1)} %param.7) | copy-start | bytes 42467332
  13.4 15.6 %copy-start.3 = (bf16[1,1536,1536]{2,1,0:T(8,128)(2,1)S(1)}, bf16[1,1536,1536]{2,1,0:T(8,128)(2,1)}, u32[]{:S(2)}) copy-start(bf16[1,1536,1536]{2,1,0:T(8,128)(2,1)} %param.8) | copy-start | bytes 14155780
  40.1 39.1 %collective-permute-start.2 = (bf16[400,1536]{1,0:T(8,128)(2,1)S(1)}, bf16[400,1536]{1,0:T(8,128)(2,1)S(1)}, u32[]{:S(2)}, u32[]{:S(2)}) collective-permute-start(bf16[400,1536]{1,0:T(8,128)(2,1)S(1)} %far_attention.2), channel_id=1, source_target_pairs={{0,29},{1,18},{2,19},{3,16},{4,17},{5,22},{6,23},{7,20},{8,21},{9,... | collective-permute-start | bytes 3686408 | tf_op jit(solution)/shard_map/ppermute | solution.py:279
  48.5 33.6 %copy-start.6 = (f32[1,1536]{1,0:T(1,128)S(1)}, f32[1,1536]{1,0:T(1,128)}, u32[]{:S(2)}) copy-start(f32[1,1536]{1,0:T(1,128)} %refs_2_.1) | copy-start | bytes 18436
  48.5 17.5 %collective-permute-start.5 = (bf16[192,1536]{1,0:T(8,128)(2,1)S(1)}, bf16[192,1536]{1,0:T(8,128)(2,1)S(1)}, u32[]{:S(2)}, u32[]{:S(2)}) collective-permute-start(bf16[192,1536]{1,0:T(8,128)(2,1)S(1)} %get-tuple-element.22), channel_id=1, source_target_pairs={{0,18},{1,29},{2,16},{3,19},{4,22},{5,17},{6,20},{7,23},{8,26},{9,... | collective-permute-start | bytes 1769480 | tf_op jit(solution)/shard_map/ppermute | solution.py:279
  48.7 28.5 %collective-permute-start.3 = (bf16[192,1536]{1,0:T(8,128)(2,1)S(1)}, bf16[192,1536]{1,0:T(8,128)(2,1)S(1)}, u32[]{:S(2)}, u32[]{:S(2)}) collective-permute-start(bf16[192,1536]{1,0:T(8,128)(2,1)S(1)} %get-tuple-element.23), channel_id=1, source_target_pairs={{0,18},{1,29},{2,16},{3,19},{4,22},{5,17},{6,20},{7,23},{8,26},{9,... | collective-permute-start | bytes 1769480 | tf_op jit(solution)/shard_map/ppermute | solution.py:279
  66.0 32.3 %collective-permute-start.6 = (bf16[192,1536]{1,0:T(8,128)(2,1)S(1)}, bf16[192,1536]{1,0:T(8,128)(2,1)S(1)}, u32[]{:S(2)}, u32[]{:S(2)}) collective-permute-start(bf16[192,1536]{1,0:T(8,128)(2,1)S(1)} %collective-permute-done.5), channel_id=1, source_target_pairs={{16,16},{17,17},{18,18},{19,19},{20,20},{21,21},{22,22},{23,23},{2... | collective-permute-start | bytes 1769480 | tf_op jit(solution)/shard_map/ppermute | solution.py:279
  77.2 21.2 %collective-permute-start.4 = (bf16[192,1536]{1,0:T(8,128)(2,1)S(1)}, bf16[192,1536]{1,0:T(8,128)(2,1)S(1)}, u32[]{:S(2)}, u32[]{:S(2)}) collective-permute-start(bf16[192,1536]{1,0:T(8,128)(2,1)S(1)} %collective-permute-done.3), channel_id=1, source_target_pairs={{16,16},{17,17},{18,18},{19,19},{20,20},{21,21},{22,22},{23,23},{2... | collective-permute-start | bytes 1769480 | tf_op jit(solution)/shard_map/ppermute | solution.py:279
  79.2 1.8 %collective-permute-start.9 = (bf16[128,1536]{1,0:T(8,128)(2,1)S(1)}, bf16[128,1536]{1,0:T(8,128)(2,1)S(1)}, u32[]{:S(2)}, u32[]{:S(2)}) collective-permute-start(bf16[128,1536]{1,0:T(8,128)(2,1)S(1)} %get-tuple-element.19), channel_id=1, source_target_pairs={{0,1},{1,0},{2,3},{3,2},{4,5},{5,4},{6,7},{7,6},{8,9},{9,8},{10,11... | collective-permute-start | bytes 1179656 | tf_op jit(solution)/shard_map/ppermute | solution.py:279
  79.3 2.3 %collective-permute-start.8 = (bf16[128,1536]{1,0:T(8,128)(2,1)S(1)}, bf16[128,1536]{1,0:T(8,128)(2,1)S(1)}, u32[]{:S(2)}, u32[]{:S(2)}) collective-permute-start(bf16[128,1536]{1,0:T(8,128)(2,1)S(1)} %get-tuple-element.20), channel_id=1, source_target_pairs={{0,1},{1,0},{2,3},{3,2},{4,5},{5,4},{6,7},{7,6},{8,9},{9,8},{10,11... | collective-permute-start | bytes 1179656 | tf_op jit(solution)/shard_map/ppermute | solution.py:279
  79.8 2.3 %collective-permute-start.7 = (bf16[128,1536]{1,0:T(8,128)(2,1)S(1)}, bf16[128,1536]{1,0:T(8,128)(2,1)S(1)}, u32[]{:S(2)}, u32[]{:S(2)}) collective-permute-start(bf16[128,1536]{1,0:T(8,128)(2,1)S(1)} %get-tuple-element.21), channel_id=1, source_target_pairs={{0,1},{1,0},{2,3},{3,2},{4,5},{5,4},{6,7},{7,6},{8,9},{9,8},{10,11... | collective-permute-start | bytes 1179656 | tf_op jit(solution)/shard_map/ppermute | solution.py:279
  109.6 32.1 %collective-permute-start.10 = (bf16[384,1536]{1,0:T(8,128)(2,1)S(1)}, bf16[384,1536]{1,0:T(8,128)(2,1)S(1)}, u32[]{:S(2)}, u32[]{:S(2)}) collective-permute-start(bf16[384,1536]{1,0:T(8,128)(2,1)S(1)} %far_attention.3), channel_id=1, source_target_pairs={{13,16},{2,17},{3,18},{0,19},{1,20},{6,21},{7,22},{4,23},{5,24},{1... | collective-permute-start | bytes 3538952 | tf_op jit(solution)/shard_map/ppermute | solution.py:279

commit v2 on v0

v2 whole, which is shorter than its diff:
```python
import functools
import math

import jax
import jax.numpy as jnp
from jax import lax
from jax.experimental import pallas as pl
from jax.experimental.pallas import tpu as pltpu
from jax.sharding import PartitionSpec as P

HEADS = 12
HD = 128
D = 1536
TS = 384
NBR = 3
HALF = TS // 2
THIRD = TS // 3
WIDE = 512
N_TILE = 16
N_SECTION = 8
PAIR = 2 * HD
PAIRS = HEADS // 2
SCALE = HD ** (-0.5) * math.log2(math.e)
OFF = -1e30
BOTH = ("section", "tile")
UNROLL = False
NEAR_VMEM = 14 * 2**20
FAR_VMEM = 14 * 2**20
NEAR_FLOPS = 0
FAR_FLOPS = 0


def normalize(hidden, gain):
    widened = hidden.astype(jnp.float32)
    square = jnp.mean(widened * widened, axis=-1, keepdims=True)
    return (widened * lax.rsqrt(square + 1e-06) * gain).astype(jnp.bfloat16)


def dot(a, b):
    return jnp.dot(a, b, preferred_element_type=jnp.float32)


def dot_t(a, b):
    return lax.dot_general(a, b, (((1,), (1,)), ((), ())), preferred_element_type=jnp.float32)


def columns(j, first=0):
    return pl.ds(pl.multiple_of(first + j * PAIR, PAIR), PAIR)


def switch(on):
    return jnp.where(on, 0.0, OFF)


def uses(lists_ref, counts_ref):
    tile = lax.axis_index("tile")
    side = 2 * (tile % 2)

    def listed(neighbour):
        found = [(lists_ref[0, j] == neighbour) & (counts_ref[0] > j) for j in range(NBR)]
        return found[0] | found[1] | found[2]

    return listed(tile + 1 - side), listed(tile - 1 + side)


def guarded(run, turn):
    if turn is None:
        run()
    else:
        pl.when(lax.axis_index("section") % 2 == turn)(run)


def near_kernel(turn, count, lists_ref, counts_ref, own_ref, *refs):
    near_refs, (gain_ref, w_ref, _, q_ref, o_ref, lse_ref, normed, kept_k, kept_v) = refs[:count], refs[count:]

    def run():
        normed[:TS, :] = normalize(own_ref[:TS, :], gain_ref[...])
        rows = TS // count
        for i, ref in enumerate(near_refs):
            normed[TS + i * rows : TS + (i + 1) * rows, :] = normalize(ref[:rows, :], gain_ref[...])
        if own_ref.shape[0] > TS:
            bias = switch(own_ref[TS : TS + 8, :HD].astype(jnp.float32) > 0)[:1, :1]
        else:
            bias = switch(uses(lists_ref, counts_ref)[0])
        lane = lax.broadcasted_iota(jnp.int32, lse_ref.shape, 1)
        lse_ref[...] = jnp.zeros_like(lse_ref)
        for head in range(2):
            kept_v[:, :, head * PAIR + HD : (head + 1) * PAIR] = jnp.ones((2, 2 * TS, HD), jnp.bfloat16)

        def project_q(j):
            q_ref[:, columns(j)] = (dot(normed[:TS, :], w_ref[:, columns(j)]) * SCALE).astype(jnp.bfloat16)

        def project_k(j, slot):
            kept_k[slot] = dot(normed[...], w_ref[:, columns(j, D)]).astype(jnp.bfloat16)

        def project_v(j, slot):
            v = dot(normed[...], w_ref[:, columns(j, 2 * D)]).astype(jnp.bfloat16)
            kept_v[slot, :, :HD] = v[:, :HD]
            kept_v[slot, :, PAIR : PAIR + HD] = v[:, HD:]

        def score(q, k, i):
            return dot_t(q[:, i * HD : (i + 1) * HD], k[:, i * HD : (i + 1) * HD])

        def weigh(s):
            s0, s1 = s[:, :TS], s[:, TS:]
            m = jnp.maximum(jnp.max(s0, axis=1, keepdims=True), jnp.max(s1, axis=1, keepdims=True) + bias)
            p0 = jnp.exp2(s0 - m).astype(jnp.bfloat16)
            p1 = jnp.exp2(s1 - (m - bias)).astype(jnp.bfloat16)
            return jnp.concatenate([p0, p1], axis=1), m

        def collect(p, m, v, j, i):
            mixed = dot(p, v[:, i * PAIR : (i + 1) * PAIR])
            total = mixed[:, HD:]
            first = pl.multiple_of(j * PAIR, PAIR) + i * HD
            o_ref[:, pl.ds(first, HD)] = mixed[:, :HD] / total
            lse_ref[...] = jnp.where(lane == 2 * j + i, m + jnp.log2(total), lse_ref[...])

        project_q(0)
        project_k(0, 0)
        project_v(0, 0)

        def step(j, more):
            slot = j % 2
            q, k, v = q_ref[:, columns(j)], kept_k[slot], kept_v[slot]
            s0 = score(q, k, 0)
            if more:
                project_q(j + 1)
            p0, m0 = weigh(s0)
            s1 = score(q, k, 1)
            if more:
                project_k(j + 1, 1 - slot)
            p1, m1 = weigh(s1)
            collect(p0, m0, v, j, 0)
            if more:
                project_v(j + 1, 1 - slot)
            collect(p1, m1, v, j, 1)

        steps(step)

    guarded(run, turn)


def steps(step):
    if UNROLL:
        for j in range(PAIRS - 1):
            step(j, True)
    else:
        lax.fori_loop(0, PAIRS - 1, lambda j, carry: step(j, True) or carry, 0)
    step(PAIRS - 1, False)


def far_kernel(turn, count, lists_ref, counts_ref, own_ref, *refs):
    far_refs, refs = refs[:count], refs[count:]
    gain_ref, q_ref, o_ref, lse_ref, w_ref, wo_ref, out_ref, normed, mixed, kept_k, kept_v = refs

    def run():
        rows = TS // count
        for i, ref in enumerate(far_refs):
            normed[i * rows : (i + 1) * rows, :] = normalize(ref[:rows, :], gain_ref[...])
        if own_ref.shape[0] > TS:
            bias = switch(own_ref[TS + 8 :, :HD].astype(jnp.float32) > 0)[:1, :1]
        else:
            beside, beyond = uses(lists_ref, counts_ref)
            bias = switch(beyond)
            out_ref[TS : TS + 8, :] = jnp.full((8, D), jnp.where(beyond, 1.0, 0.0)).astype(jnp.bfloat16)
            out_ref[TS + 8 :, :] = jnp.full((8, D), jnp.where(beside, 1.0, 0.0)).astype(jnp.bfloat16)
        lane = lax.broadcasted_iota(jnp.int32, lse_ref.shape, 1)
        for head in range(2):
            kept_v[:, :, head * PAIR + HD : (head + 1) * PAIR] = jnp.ones((2, TS, HD), jnp.bfloat16)

        def project_k(j, slot):
            kept_k[slot] = dot(normed[...], w_ref[:, columns(j, D)]).astype(jnp.bfloat16)

        def project_v(j, slot):
            v = dot(normed[...], w_ref[:, columns(j, 2 * D)]).astype(jnp.bfloat16)
            kept_v[slot, :, :HD] = v[:, :HD]
            kept_v[slot, :, PAIR : PAIR + HD] = v[:, HD:]

        def score(q, k, i):
            return dot_t(q[:, i * HD : (i + 1) * HD], k[:, i * HD : (i + 1) * HD])

        def weigh(s):
            m = jnp.max(s, axis=1, keepdims=True)
            return jnp.exp2(s - m).astype(jnp.bfloat16), m + bias

        def collect(p, m, v, j, i):
            both = dot(p, v[:, i * PAIR : (i + 1) * PAIR])
            before = jnp.sum(jnp.where(lane == 2 * j + i, lse_ref[...], 0.0), axis=1, keepdims=True)
            top = jnp.maximum(before, m)
            w0, w1 = jnp.exp2(before - top), jnp.exp2(m - top)
            first = pl.multiple_of(j * PAIR, PAIR) + i * HD
            o = (o_ref[:, pl.ds(first, HD)] * w0 + both[:, :HD] * w1) / (w0 + both[:, HD:] * w1)
            mixed[:, pl.ds(first, HD)] = o.astype(jnp.bfloat16)

        project_k(0, 0)
        project_v(0, 0)

        def step(j, more):
            slot = j % 2
            q, k, v = q_ref[:, columns(j)], kept_k[slot], kept_v[slot]
            s0 = score(q, k, 0)
            s1 = score(q, k, 1)
            p0, m0 = weigh(s0)
            if more:
                project_k(j + 1, 1 - slot)
            p1, m1 = weigh(s1)
            collect(p0, m0, v, j, 0)
            if more:
                project_v(j + 1, 1 - slot)
            collect(p1, m1, v, j, 1)

        steps(step)

        def finish(j, carry):
            cut = pl.ds(pl.multiple_of(j * WIDE, WIDE), WIDE)
            update = dot(mixed[...], wo_ref[:, cut])
            out_ref[:TS, cut] = (own_ref[:TS, cut].astype(jnp.float32) + update).astype(jnp.bfloat16)
            return carry

        lax.fori_loop(0, D // WIDE, finish, 0)

    guarded(run, turn)


SMEM = pl.BlockSpec(memory_space=pltpu.SMEM)
VMEM = pl.BlockSpec(memory_space=pltpu.VMEM)
ANY = pl.BlockSpec(memory_space=pl.ANY)


def near_attention(turn, lists, counts, own, near, gain, wqkv, wo):
    return pl.pallas_call(
        functools.partial(near_kernel, turn, len(near)),
        out_shape=(
            jax.ShapeDtypeStruct((TS, D), jnp.bfloat16),
            jax.ShapeDtypeStruct((TS, D), jnp.float32),
            jax.ShapeDtypeStruct((TS, HD), jnp.float32),
        ),
        in_specs=[SMEM, SMEM] + [VMEM] * (4 + len(near)),
        out_specs=(VMEM, VMEM, VMEM),
        scratch_shapes=[
            pltpu.VMEM((2 * TS, D), jnp.bfloat16),
            pltpu.VMEM((2, 2 * TS, PAIR), jnp.bfloat16),
            pltpu.VMEM((2, 2 * TS, 2 * PAIR), jnp.bfloat16),
        ],
        compiler_params=pltpu.CompilerParams(vmem_limit_bytes=NEAR_VMEM),
        cost_estimate=pl.CostEstimate(flops=NEAR_FLOPS, bytes_accessed=0, transcendentals=0),
        name="near_attention",
    )(lists, counts, own, *near, gain, wqkv, wo)


def far_attention(turn, rows, lists, counts, own, far, gain, q, o, lse, wqkv, wo):
    return pl.pallas_call(
        functools.partial(far_kernel, turn, len(far)),
        out_shape=jax.ShapeDtypeStruct((rows, D), jnp.bfloat16),
        in_specs=[SMEM, SMEM] + [VMEM] * (7 + len(far)),
        out_specs=VMEM,
        scratch_shapes=[
            pltpu.VMEM((TS, D), jnp.bfloat16),
            pltpu.VMEM((TS, D), jnp.bfloat16),
            pltpu.VMEM((2, TS, PAIR), jnp.bfloat16),
            pltpu.VMEM((2, TS, 2 * PAIR), jnp.bfloat16),
        ],
        compiler_params=pltpu.CompilerParams(vmem_limit_bytes=FAR_VMEM),
        cost_estimate=pl.CostEstimate(flops=FAR_FLOPS, bytes_accessed=0, transcendentals=0),
        name="far_attention",
    )(lists, counts, own, *far, gain, q, o, lse, wqkv, wo)


def choose_kernel(a_ref, b_ref, out_ref, done):
    def move(source):
        copy = pltpu.make_async_copy(source, out_ref, done)
        copy.start()
        copy.wait()

    odd = lax.axis_index("section") % 2 == 1
    pl.when(odd)(lambda: move(b_ref))
    pl.when(jnp.logical_not(odd))(lambda: move(a_ref.at[pl.ds(0, TS)]))


def choose(a, b):
    return pl.pallas_call(
        choose_kernel,
        out_shape=jax.ShapeDtypeStruct((TS, D), jnp.bfloat16),
        in_specs=[VMEM, VMEM],
        out_specs=ANY,
        scratch_shapes=[pltpu.SemaphoreType.DMA],
        compiler_params=pltpu.CompilerParams(vmem_limit_bytes=NEAR_VMEM),
        name="choose",
    )(a, b)


def place(t):
    z, r = divmod(t, 4)
    if r == 0:
        return 4 * ((z - 1) % 4) + 1
    if r == 3:
        return 4 * z
    return 4 * z + 1 + r


def other(t):
    return t + 1 if t % 2 else t - 1


def route(moves, sections, step):
    return [(s * N_TILE + a, (s + step) % N_SECTION * N_TILE + b) for s in sections for a, b in moves]


TILES = range(N_TILE)
ALL, EVEN, ODD = range(N_SECTION), range(0, N_SECTION, 2), range(1, N_SECTION, 2)
SWAP = [(t, t ^ 1) for t in TILES]
SPREAD = [(t, place(t)) for t in TILES]
SPREAD_PAIR = [(t, place(t ^ 1)) for t in TILES]
STAY = [(t, t) for t in TILES]
GATHER = [(place(t), t) for t in TILES]
NEXT_CHIP = route([(t, other(t)) for t in TILES if 0 <= other(t) < N_TILE], ALL, 0)


def pieces(block, rows):
    return [block[i : i + rows] for i in range(0, TS, rows)]


def on_device(latents, wqkv, wo, gains, lists, counts):
    own = latents[0]
    wqkv, wo = wqkv[0], wo[0]

    def send(blocks, *route_of):
        perm = route(*route_of)
        return [lax.ppermute(block, BOTH, perm) for block in blocks]

    far = [lax.ppermute(own, BOTH, NEXT_CHIP)]
    near = send([own], SWAP, ALL, 0)
    q, o, lse = near_attention(None, lists, counts, own, near, gains, wqkv, wo)
    own = far_attention(None, TS + 16, lists, counts, own, far, gains, q, o, lse, wqkv, wo)

    (own_a,) = send([own], SPREAD, EVEN, 1)
    (own_b,) = send([own], SPREAD, ODD, 1)
    (turned,) = send([own], SPREAD_PAIR, ODD, -1)
    own, own_a = lax.optimization_barrier((own, own_a))
    far_a = send([own[:TS]], SPREAD_PAIR, EVEN, 1)

    near_a = send([own_a[:TS]], SWAP, ODD, 0)
    q, o, lse = near_attention(1, lists, counts, own_a, near_a, gains, wqkv, wo)
    turned, lse = lax.optimization_barrier((turned, lse))
    far_b = send([turned], STAY, EVEN, 2)
    done_a = far_attention(1, TS + 16, lists, counts, own_a, far_a, gains, q, o, lse, wqkv, wo)
    own_b, done_a = lax.optimization_barrier((own_b, done_a))
    (home_a,) = send([done_a], GATHER, ODD, 1)

    near_b = send([own_b[:TS]], SWAP, EVEN, 0)
    q, o, lse = near_attention(0, lists, counts, own_b, near_b, gains, wqkv, wo)
    done_b = far_attention(0, TS, lists, counts, own_b, far_b, gains, q, o, lse, wqkv, wo)
    (home_b,) = send([done_b], GATHER, EVEN, 1)
    return choose(home_a, home_b)[None]


def solution(mesh):
    return jax.shard_map(
        on_device,
        mesh=mesh,
        in_specs=(
            P("section", "tile", None),
            P("section", None, None),
            P("section", None, None),
            P("section", None),
            P("tile", None),
            P("tile"),
        ),
        out_specs=P("section", "tile", None),
        check_vma=False,
    )
```

time: 147 us -> 141 us (0.959)
  the two profiles are of different devices: /device:TPU:0 before, /device:TPU:8 now
where the time goes in v2:
time: 141 us; the launch traced here: 140 us
  Pallas kernels  56.6 us (40%)
  waiting for transfers between devices  47.8 us (34%)
  starting transfers between devices  24.5 us (17%)
  local copies, waits for them, and re-layouts  10.2 us (7%)
    ppermute x10, waiting for transfers between devices, send(): return [lax.ppermute(block, BOTH, perm) for block in blocks]  47.8 us
    pallas_call x3, Pallas kernels, near_attention(): pl.pallas_call(functools.partial(near_kernel, turn, len(near)), out_shape...  32.7 us
    ppermute x10, starting transfers between devices, send(): return [lax.ppermute(block, BOTH, perm) for block in blocks]  23.8 us
    pallas_call x3, Pallas kernels, far_attention(): pl.pallas_call(functools.partial(far_kernel, turn, len(far)), out_shape=j...  22.9 us
    unnamed x18, local copies, waits for them, and re-layouts  10 us
  transfers between devices with their start and end apart: 11, of which 5 were waited for; matrix products, arithmetic and copies ran while one was open for 0% of the time, Pallas kernels for 32%

profile of v2, /device:TPU:8, one launch (start us, length us, event | category | flops | bytes accessed | tf_op | source)
XLA Modules:
  0.0 140.1 jit_solution(5837818839600839646)
XLA Ops:
  0.0 0.7 collective-permute-start
  1.4 1.7 %collective-permute-done.1.refs_0_ = bf16[384,1536]{1,0:T(8,128)(2,1)S(1)} collective-permute-done((bf16[384,1536]{1,0:T(8,128)(2,1)}, bf16[384,1536]{1,0:T(8,128)(2,1)S(1)}, u32[]{:S(2)}, u32[]{:S(2)}) %collective-permute-start.1) | collective-permute-done | bytes 1179680 | tf_op jit(solution)/shard_map/ppermute | solution.py:329
  3.1 5.0 %copy-done = bf16[1,1536,4608]{2,1,0:T(8,128)(2,1)S(1)} copy-done((bf16[1,1536,4608]{2,1,0:T(8,128)(2,1)S(1)}, bf16[1,1536,4608]{2,1,0:T(8,128)(2,1)}, u32[]{:S(2)}) %copy-start) | copy-done | bytes 14155800
  8.1 2.3 %copy-done.2 = bf16[1,1536,1536]{2,1,0:T(8,128)(2,1)S(1)} copy-done((bf16[1,1536,1536]{2,1,0:T(8,128)(2,1)S(1)}, bf16[1,1536,1536]{2,1,0:T(8,128)(2,1)}, u32[]{:S(2)}) %copy-start.2) | copy-done | bytes 4718616
  10.4 1.3 copy-done.4
  13.0 15.5 %near_attention.3 = (bf16[384,1536]{1,0:T(8,128)(2,1)S(1)}, f32[384,1536]{1,0:T(8,128)S(1)}, f32[384,128]{1,0:T(8,128)S(1)}) custom-call(s32[1,3]{1,0:T(1,128)S(1)} %copy-done.7, s32[1]{0:T(128)S(6)} %copy.7.counts_ref, bf16[384,1536]{1,0:T(8,128)(2,1)S(1)} %bitcast.18, bf16[384,1536]{1,0:T(8,128)(2,1)S(1)} %collective-permute-done.1.refs_0_, ...), custom_call_target="tpu_custom_call" | custom-call | tf_op jit(solution)/shard_map/near_attention/pallas_call | solution.py:231
  28.6 11.1 %far_attention.3 = bf16[400,1536]{1,0:T(8,128)(2,1)S(1)} custom-call(s32[1,3]{1,0:T(1,128)S(1)} %copy-done.7, s32[1]{0:T(128)S(6)} %copy.7.counts_ref, bf16[384,1536]{1,0:T(8,128)(2,1)S(1)} %bitcast.19, bf16[384,1536]{1,0:T(8,128)(2,1)S(1)} %collective-permute-done.refs_0_, f32[1,1536]{1,0:T(1,128)S(1)} %copy-done.5, ...), custom_call_target="tpu_custom_call" | custom-call | tf_op jit(solution)/shard_map/far_attention/pallas_call | solution.py:252
  39.7 1.3 collective-permute-start.3
  41.0 9.6 %collective-permute-start.6 = (bf16[400,1536]{1,0:T(8,128)(2,1)S(1)}, bf16[400,1536]{1,0:T(8,128)(2,1)S(1)}, u32[]{:S(2)}, u32[]{:S(2)}) collective-permute-start(bf16[400,1536]{1,0:T(8,128)(2,1)S(1)} %far_attention.3), channel_id=1, source_target_pairs={{16,2},{17,13},{18,0},{19,3},{20,6},{21,1},{22,4},{23,7},{24,10},{... | collective-permute-start | bytes 3686408 | tf_op jit(solution)/shard_map/ppermute | solution.py:329
  50.6 4.8 %collective-permute-start.2 = (bf16[400,1536]{1,0:T(8,128)(2,1)S(1)}, bf16[400,1536]{1,0:T(8,128)(2,1)S(1)}, u32[]{:S(2)}, u32[]{:S(2)}) collective-permute-start(bf16[400,1536]{1,0:T(8,128)(2,1)S(1)} %far_attention.3), channel_id=1, source_target_pairs={{16,45},{17,34},{18,35},{19,32},{20,33},{21,38},{22,39},{23,36},{2... | collective-permute-start | bytes 3686408 | tf_op jit(solution)/shard_map/ppermute | solution.py:329
  55.4 5.6 %collective-permute-done.3.own_ref = bf16[400,1536]{1,0:T(8,128)(2,1)S(1)} collective-permute-done((bf16[400,1536]{1,0:T(8,128)(2,1)S(1)}, bf16[400,1536]{1,0:T(8,128)(2,1)S(1)}, u32[]{:S(2)}, u32[]{:S(2)}) %collective-permute-start.3) | collective-permute-done | bytes 1228832 | tf_op jit(solution)/shard_map/ppermute | solution.py:329
  61.1 2.7 %collective-permute-start.5 = (bf16[384,1536]{1,0:T(8,128)(2,1)S(1)}, bf16[384,1536]{1,0:T(8,128)(2,1)S(1)}, u32[]{:S(2)}, u32[]{:S(2)}) collective-permute-start(bf16[384,1536]{1,0:T(8,128)(2,1)S(1)} %slice.10), channel_id=1, source_target_pairs={{16,17},{17,16},{18,19},{19,18},{20,21},{21,20},{22,23},{23,22},{2... | collective-permute-start | bytes 3538952 | tf_op jit(solution)/shard_map/ppermute | solution.py:329
  63.9 1.3 collective-permute-start.4
  65.2 1.1 collective-permute-done.5.refs_0_
  66.3 16.4 %near_attention.4 = (bf16[384,1536]{1,0:T(8,128)(2,1)S(1)}, f32[384,1536]{1,0:T(8,128)S(1)}, f32[384,128]{1,0:T(8,128)S(1)}) custom-call(s32[1,3]{1,0:T(1,128)S(1)} %copy-done.8, s32[1]{0:T(128)S(6)} %copy.7.counts_ref, bf16[400,1536]{1,0:T(8,128)(2,1)S(1)} %collective-permute-done.3.own_ref, bf16[384,1536]{1,0:T(8,128)(2,1)S(1)} %collective-permute-done.5.refs_0_, ...), custom_call_target="tpu_custom_call" | custom-call | tf_op jit(solution)/shard_map/near_attention/pallas_call | solution.py:231
  82.7 0.7 collective-permute-start.8
  83.4 11.2 %far_attention.4 = bf16[400,1536]{1,0:T(8,128)(2,1)S(1)} custom-call(s32[1,3]{1,0:T(1,128)S(1)} %copy-done.8, s32[1]{0:T(128)S(6)} %copy.7.counts_ref, bf16[400,1536]{1,0:T(8,128)(2,1)S(1)} %collective-permute-done.3.own_ref, bf16[384,1536]{1,0:T(8,128)(2,1)S(1)} %collective-permute-done.4.refs_0_, f32[1,1536]{1,0:T(1,128)S(1)} %copy-done.6, ...), custom_call_target="tpu_custom_call" | custom-call | tf_op jit(solution)/shard_map/far_attention/pallas_call | solution.py:252
  94.8 0.7 collective-permute-start.9
  95.5 1.4 collective-permute-start.7
  96.9 0.8 near_attention.5
  98.3 1.3 collective-permute-start.10
  99.6 24.3 %collective-permute-done.7.a_ref = bf16[400,1536]{1,0:T(8,128)(2,1)S(1)} collective-permute-done((bf16[400,1536]{1,0:T(8,128)(2,1)S(1)}, bf16[400,1536]{1,0:T(8,128)(2,1)S(1)}, u32[]{:S(2)}, u32[]{:S(2)}) %collective-permute-start.7) | collective-permute-done | bytes 1228832 | tf_op jit(solution)/shard_map/ppermute | solution.py:329
  123.9 15.0 %collective-permute-done.10.b_ref = bf16[384,1536]{1,0:T(8,128)(2,1)S(1)} collective-permute-done((bf16[384,1536]{1,0:T(8,128)(2,1)S(1)}, bf16[384,1536]{1,0:T(8,128)(2,1)S(1)}, u32[]{:S(2)}, u32[]{:S(2)}) %collective-permute-start.10) | collective-permute-done | bytes 1179680 | tf_op jit(solution)/shard_map/ppermute | solution.py:329
  138.9 1.0 choose.1
  (26 shorter events, 2.2 us)
Async XLA Ops:
  0.0 3.1 %collective-permute-start.1 = (bf16[384,1536]{1,0:T(8,128)(2,1)}, bf16[384,1536]{1,0:T(8,128)(2,1)S(1)}, u32[]{:S(2)}, u32[]{:S(2)}) collective-permute-start(bf16[384,1536]{1,0:T(8,128)(2,1)} %bitcast.16), channel_id=1, source_target_pairs={{0,1},{1,0},{2,3},{3,2},{4,5},{5,4},{6,7},{7,6},{8,9},{9,8},{10,11... | collective-permute-start | bytes 3538952 | tf_op jit(solution)/shard_map/ppermute | solution.py:329
  0.0 28.6 %collective-permute-start = (bf16[384,1536]{1,0:T(8,128)(2,1)}, bf16[384,1536]{1,0:T(8,128)(2,1)S(1)}, u32[]{:S(2)}, u32[]{:S(2)}) collective-permute-start(bf16[384,1536]{1,0:T(8,128)(2,1)} %bitcast.17), channel_id=1, source_target_pairs={{1,2},{2,1},{3,4},{4,3},{5,6},{6,5},{7,8},{8,7},{9,10},{10,9},{11,... | collective-permute-start | bytes 3538952 | tf_op jit(solution)/shard_map/ppermute | solution.py:331
  3.1 5.0 %copy-start = (bf16[1,1536,4608]{2,1,0:T(8,128)(2,1)S(1)}, bf16[1,1536,4608]{2,1,0:T(8,128)(2,1)}, u32[]{:S(2)}) copy-start(bf16[1,1536,4608]{2,1,0:T(8,128)(2,1)} %param.7) | copy-start | bytes 42467332
  8.1 2.3 %copy-start.2 = (bf16[1,1536,1536]{2,1,0:T(8,128)(2,1)S(1)}, bf16[1,1536,1536]{2,1,0:T(8,128)(2,1)}, u32[]{:S(2)}) copy-start(bf16[1,1536,1536]{2,1,0:T(8,128)(2,1)} %param.8) | copy-start | bytes 14155780
  10.4 1.3 copy-start.4
  11.7 0.7 copy-start.5
  12.4 0.7 copy-start.7
  13.0 15.6 %copy-start.1 = (bf16[1,1536,4608]{2,1,0:T(8,128)(2,1)S(1)}, bf16[1,1536,4608]{2,1,0:T(8,128)(2,1)}, u32[]{:S(2)}) copy-start(bf16[1,1536,4608]{2,1,0:T(8,128)(2,1)} %param.7) | copy-start | bytes 42467332
  13.0 15.6 %copy-start.3 = (bf16[1,1536,1536]{2,1,0:T(8,128)(2,1)S(1)}, bf16[1,1536,1536]{2,1,0:T(8,128)(2,1)}, u32[]{:S(2)}) copy-start(bf16[1,1536,1536]{2,1,0:T(8,128)(2,1)} %param.8) | copy-start | bytes 14155780
  39.7 21.3 %collective-permute-start.3 = (bf16[400,1536]{1,0:T(8,128)(2,1)S(1)}, bf16[400,1536]{1,0:T(8,128)(2,1)S(1)}, u32[]{:S(2)}, u32[]{:S(2)}) collective-permute-start(bf16[400,1536]{1,0:T(8,128)(2,1)S(1)} %far_attention.3), channel_id=1, source_target_pairs={{0,29},{1,18},{2,19},{3,16},{4,17},{5,22},{6,23},{7,20},{8,21},{9,... | collective-permute-start | bytes 3686408 | tf_op jit(solution)/shard_map/ppermute | solution.py:329
  41.0 41.7 %collective-permute-start.6 = (bf16[400,1536]{1,0:T(8,128)(2,1)S(1)}, bf16[400,1536]{1,0:T(8,128)(2,1)S(1)}, u32[]{:S(2)}, u32[]{:S(2)}) collective-permute-start(bf16[400,1536]{1,0:T(8,128)(2,1)S(1)} %far_attention.3), channel_id=1, source_target_pairs={{16,2},{17,13},{18,0},{19,3},{20,6},{21,1},{22,4},{23,7},{24,10},{... | collective-permute-start | bytes 3686408 | tf_op jit(solution)/shard_map/ppermute | solution.py:329
  50.6 44.1 %collective-permute-start.2 = (bf16[400,1536]{1,0:T(8,128)(2,1)S(1)}, bf16[400,1536]{1,0:T(8,128)(2,1)S(1)}, u32[]{:S(2)}, u32[]{:S(2)}) collective-permute-start(bf16[400,1536]{1,0:T(8,128)(2,1)S(1)} %far_attention.3), channel_id=1, source_target_pairs={{16,45},{17,34},{18,35},{19,32},{20,33},{21,38},{22,39},{23,36},{2... | collective-permute-start | bytes 3686408 | tf_op jit(solution)/shard_map/ppermute | solution.py:329
  61.1 5.2 %copy-start.6 = (f32[1,1536]{1,0:T(1,128)S(1)}, f32[1,1536]{1,0:T(1,128)}, u32[]{:S(2)}) copy-start(f32[1,1536]{1,0:T(1,128)} %refs_1_.11) | copy-start | bytes 18436
  61.1 5.2 %copy-start.8 = (s32[1,3]{1,0:T(1,128)S(1)}, s32[1,3]{1,0:T(1,128)}, u32[]{:S(2)}) copy-start(s32[1,3]{1,0:T(1,128)} %lists_ref.11) | copy-start | bytes 40
  61.1 5.2 %collective-permute-start.5 = (bf16[384,1536]{1,0:T(8,128)(2,1)S(1)}, bf16[384,1536]{1,0:T(8,128)(2,1)S(1)}, u32[]{:S(2)}, u32[]{:S(2)}) collective-permute-start(bf16[384,1536]{1,0:T(8,128)(2,1)S(1)} %slice.10), channel_id=1, source_target_pairs={{16,17},{17,16},{18,19},{19,18},{20,21},{21,20},{22,23},{23,22},{2... | collective-permute-start | bytes 3538952 | tf_op jit(solution)/shard_map/ppermute | solution.py:329
  63.9 19.5 %collective-permute-start.4 = (bf16[384,1536]{1,0:T(8,128)(2,1)S(1)}, bf16[384,1536]{1,0:T(8,128)(2,1)S(1)}, u32[]{:S(2)}, u32[]{:S(2)}) collective-permute-start(bf16[384,1536]{1,0:T(8,128)(2,1)S(1)} %slice.9), channel_id=1, source_target_pairs={{0,18},{1,29},{2,16},{3,19},{4,22},{5,17},{6,20},{7,23},{8,26},{9,... | collective-permute-start | bytes 3538952 | tf_op jit(solution)/shard_map/ppermute | solution.py:329
  82.7 15.0 %collective-permute-start.8 = (bf16[400,1536]{1,0:T(8,128)(2,1)S(1)}, bf16[400,1536]{1,0:T(8,128)(2,1)S(1)}, u32[]{:S(2)}, u32[]{:S(2)}) collective-permute-start(bf16[400,1536]{1,0:T(8,128)(2,1)S(1)} %collective-permute-done.6), channel_id=1, source_target_pairs={{0,32},{1,33},{2,34},{3,35},{4,36},{5,37},{6,38},{7,39},{8,40},{9,... | collective-permute-start | bytes 3686408 | tf_op jit(solution)/shard_map/ppermute | solution.py:329
  94.8 2.1 %collective-permute-start.9 = (bf16[384,1536]{1,0:T(8,128)(2,1)S(1)}, bf16[384,1536]{1,0:T(8,128)(2,1)S(1)}, u32[]{:S(2)}, u32[]{:S(2)}) collective-permute-start(bf16[384,1536]{1,0:T(8,128)(2,1)S(1)} %slice.11), channel_id=1, source_target_pairs={{0,1},{1,0},{2,3},{3,2},{4,5},{5,4},{6,7},{7,6},{8,9},{9,8},{10,11... | collective-permute-start | bytes 3538952 | tf_op jit(solution)/shard_map/ppermute | solution.py:329
  95.5 28.4 %collective-permute-start.7 = (bf16[400,1536]{1,0:T(8,128)(2,1)S(1)}, bf16[400,1536]{1,0:T(8,128)(2,1)S(1)}, u32[]{:S(2)}, u32[]{:S(2)}) collective-permute-start(bf16[400,1536]{1,0:T(8,128)(2,1)S(1)} %far_attention.4), channel_id=1, source_target_pairs={{29,32},{18,33},{19,34},{16,35},{17,36},{22,37},{23,38},{20,39},{2... | collective-permute-start | bytes 3686408 | tf_op jit(solution)/shard_map/ppermute | solution.py:329
  98.3 40.7 %collective-permute-start.10 = (bf16[384,1536]{1,0:T(8,128)(2,1)S(1)}, bf16[384,1536]{1,0:T(8,128)(2,1)S(1)}, u32[]{:S(2)}, u32[]{:S(2)}) collective-permute-start(bf16[384,1536]{1,0:T(8,128)(2,1)S(1)} %far_attention.5), channel_id=1, source_target_pairs={{13,16},{2,17},{3,18},{0,19},{1,20},{6,21},{7,22},{4,23},{5,24},{1... | collective-permute-start | bytes 3538952 | tf_op jit(solution)/shard_map/ppermute | solution.py:329

commit v3 on v2

--- a/solution.py
+++ b/solution.py
@@ -15,7 +15,7 @@
 NBR = 3
 HALF = TS // 2
 THIRD = TS // 3
-WIDE = 512
+WIDE = 768
 N_TILE = 16
 N_SECTION = 8
 PAIR = 2 * HD
@@ -23,7 +23,6 @@
 SCALE = HD ** (-0.5) * math.log2(math.e)
 OFF = -1e30
 BOTH = ("section", "tile")
-UNROLL = False
 NEAR_VMEM = 14 * 2**20
 FAR_VMEM = 14 * 2**20
 NEAR_FLOPS = 0
@@ -135,13 +134,13 @@
                 project_v(j + 1, 1 - slot)
             collect(p1, m1, v, j, 1)
 
-        steps(step)
+        steps(step, False)
 
     guarded(run, turn)
 
 
-def steps(step):
-    if UNROLL:
+def steps(step, straight):
+    if straight:
         for j in range(PAIRS - 1):
             step(j, True)
     else:
@@ -209,7 +208,7 @@
                 project_v(j + 1, 1 - slot)
             collect(p1, m1, v, j, 1)
 
-        steps(step)
+        steps(step, turn == 0)
 
         def finish(j, carry):
             cut = pl.ds(pl.multiple_of(j * WIDE, WIDE), WIDE)

time: 141 us -> 140 us (level)
  no operation moved by 1% of the time
where the time goes in v3:
time: 140 us
  Pallas kernels  56.6 us (40%)
  waiting for transfers between devices  47.2 us (34%)
  starting transfers between devices  24.5 us (18%)
  local copies, waits for them, and re-layouts  10.2 us (7%)
    ppermute x10, waiting for transfers between devices, send(): return [lax.ppermute(block, BOTH, perm) for block in blocks]  47.2 us
    pallas_call x3, Pallas kernels, near_attention(): pl.pallas_call(functools.partial(near_kernel, turn, len(near)), out_shape...  32.7 us
    ppermute x10, starting transfers between devices, send(): return [lax.ppermute(block, BOTH, perm) for block in blocks]  23.8 us
    pallas_call x3, Pallas kernels, far_attention(): pl.pallas_call(functools.partial(far_kernel, turn, len(far)), out_shape=j...  22.8 us
    unnamed x18, local copies, waits for them, and re-layouts  10 us
  transfers between devices with their start and end apart: 11, of which 5 were waited for; matrix products, arithmetic and copies ran while one was open for 0% of the time, Pallas kernels for 32%

profile of v3, /device:TPU:8, one launch (start us, length us, event | category | flops | bytes accessed | tf_op | source)
XLA Modules:
  0.0 139.5 jit_solution(13140692217418962590)
XLA Ops:
  1.4 1.7 %collective-permute-done.1.refs_0_ = bf16[384,1536]{1,0:T(8,128)(2,1)S(1)} collective-permute-done((bf16[384,1536]{1,0:T(8,128)(2,1)}, bf16[384,1536]{1,0:T(8,128)(2,1)S(1)}, u32[]{:S(2)}, u32[]{:S(2)}) %collective-permute-start.1) | collective-permute-done | bytes 1179680 | tf_op jit(solution)/shard_map/ppermute | solution.py:328
  3.1 5.0 %copy-done = bf16[1,1536,4608]{2,1,0:T(8,128)(2,1)S(1)} copy-done((bf16[1,1536,4608]{2,1,0:T(8,128)(2,1)S(1)}, bf16[1,1536,4608]{2,1,0:T(8,128)(2,1)}, u32[]{:S(2)}) %copy-start) | copy-done | bytes 14155800
  8.1 2.3 %copy-done.2 = bf16[1,1536,1536]{2,1,0:T(8,128)(2,1)S(1)} copy-done((bf16[1,1536,1536]{2,1,0:T(8,128)(2,1)S(1)}, bf16[1,1536,1536]{2,1,0:T(8,128)(2,1)}, u32[]{:S(2)}) %copy-start.2) | copy-done | bytes 4718616
  10.4 1.3 copy-done.4
  13.0 15.5 %near_attention.3 = (bf16[384,1536]{1,0:T(8,128)(2,1)S(1)}, f32[384,1536]{1,0:T(8,128)S(1)}, f32[384,128]{1,0:T(8,128)S(1)}) custom-call(s32[1,3]{1,0:T(1,128)S(1)} %copy-done.7, s32[1]{0:T(128)S(6)} %copy.7.counts_ref, bf16[384,1536]{1,0:T(8,128)(2,1)S(1)} %bitcast.18, bf16[384,1536]{1,0:T(8,128)(2,1)S(1)} %collective-permute-done.1.refs_0_, ...), custom_call_target="tpu_custom_call" | custom-call | tf_op jit(solution)/shard_map/near_attention/pallas_call | solution.py:230
  28.6 10.9 %far_attention.3 = bf16[400,1536]{1,0:T(8,128)(2,1)S(1)} custom-call(s32[1,3]{1,0:T(1,128)S(1)} %copy-done.7, s32[1]{0:T(128)S(6)} %copy.7.counts_ref, bf16[384,1536]{1,0:T(8,128)(2,1)S(1)} %bitcast.19, bf16[384,1536]{1,0:T(8,128)(2,1)S(1)} %collective-permute-done.refs_0_, f32[1,1536]{1,0:T(1,128)S(1)} %copy-done.5, ...), custom_call_target="tpu_custom_call" | custom-call | tf_op jit(solution)/shard_map/far_attention/pallas_call | solution.py:251
  39.5 1.3 collective-permute-start.3
  40.8 9.6 %collective-permute-start.6 = (bf16[400,1536]{1,0:T(8,128)(2,1)S(1)}, bf16[400,1536]{1,0:T(8,128)(2,1)S(1)}, u32[]{:S(2)}, u32[]{:S(2)}) collective-permute-start(bf16[400,1536]{1,0:T(8,128)(2,1)S(1)} %far_attention.3), channel_id=1, source_target_pairs={{16,2},{17,13},{18,0},{19,3},{20,6},{21,1},{22,4},{23,7},{24,10},{... | collective-permute-start | bytes 3686408 | tf_op jit(solution)/shard_map/ppermute | solution.py:328
  50.4 4.8 %collective-permute-start.2 = (bf16[400,1536]{1,0:T(8,128)(2,1)S(1)}, bf16[400,1536]{1,0:T(8,128)(2,1)S(1)}, u32[]{:S(2)}, u32[]{:S(2)}) collective-permute-start(bf16[400,1536]{1,0:T(8,128)(2,1)S(1)} %far_attention.3), channel_id=1, source_target_pairs={{16,45},{17,34},{18,35},{19,32},{20,33},{21,38},{22,39},{23,36},{2... | collective-permute-start | bytes 3686408 | tf_op jit(solution)/shard_map/ppermute | solution.py:328
  55.2 5.6 %collective-permute-done.3.own_ref = bf16[400,1536]{1,0:T(8,128)(2,1)S(1)} collective-permute-done((bf16[400,1536]{1,0:T(8,128)(2,1)S(1)}, bf16[400,1536]{1,0:T(8,128)(2,1)S(1)}, u32[]{:S(2)}, u32[]{:S(2)}) %collective-permute-start.3) | collective-permute-done | bytes 1228832 | tf_op jit(solution)/shard_map/ppermute | solution.py:328
  60.9 2.7 %collective-permute-start.5 = (bf16[384,1536]{1,0:T(8,128)(2,1)S(1)}, bf16[384,1536]{1,0:T(8,128)(2,1)S(1)}, u32[]{:S(2)}, u32[]{:S(2)}) collective-permute-start(bf16[384,1536]{1,0:T(8,128)(2,1)S(1)} %slice.10), channel_id=1, source_target_pairs={{16,17},{17,16},{18,19},{19,18},{20,21},{21,20},{22,23},{23,22},{2... | collective-permute-start | bytes 3538952 | tf_op jit(solution)/shard_map/ppermute | solution.py:328
  63.7 1.3 collective-permute-start.4
  65.0 1.1 collective-permute-done.5.refs_0_
  66.1 16.4 %near_attention.4 = (bf16[384,1536]{1,0:T(8,128)(2,1)S(1)}, f32[384,1536]{1,0:T(8,128)S(1)}, f32[384,128]{1,0:T(8,128)S(1)}) custom-call(s32[1,3]{1,0:T(1,128)S(1)} %copy-done.8, s32[1]{0:T(128)S(6)} %copy.7.counts_ref, bf16[400,1536]{1,0:T(8,128)(2,1)S(1)} %collective-permute-done.3.own_ref, bf16[384,1536]{1,0:T(8,128)(2,1)S(1)} %collective-permute-done.5.refs_0_, ...), custom_call_target="tpu_custom_call" | custom-call | tf_op jit(solution)/shard_map/near_attention/pallas_call | solution.py:230
  82.5 0.7 collective-permute-start.8
  83.3 11.1 %far_attention.4 = bf16[400,1536]{1,0:T(8,128)(2,1)S(1)} custom-call(s32[1,3]{1,0:T(1,128)S(1)} %copy-done.8, s32[1]{0:T(128)S(6)} %copy.7.counts_ref, bf16[400,1536]{1,0:T(8,128)(2,1)S(1)} %collective-permute-done.3.own_ref, bf16[384,1536]{1,0:T(8,128)(2,1)S(1)} %collective-permute-done.4.refs_0_, f32[1,1536]{1,0:T(1,128)S(1)} %copy-done.6, ...), custom_call_target="tpu_custom_call" | custom-call | tf_op jit(solution)/shard_map/far_attention/pallas_call | solution.py:251
  94.5 0.7 collective-permute-start.9
  95.2 1.4 collective-permute-start.7
  96.6 0.8 near_attention.5
  97.4 0.8 far_attention.5
  98.2 1.3 collective-permute-start.10
  99.5 24.1 %collective-permute-done.7.a_ref = bf16[400,1536]{1,0:T(8,128)(2,1)S(1)} collective-permute-done((bf16[400,1536]{1,0:T(8,128)(2,1)S(1)}, bf16[400,1536]{1,0:T(8,128)(2,1)S(1)}, u32[]{:S(2)}, u32[]{:S(2)}) %collective-permute-start.7) | collective-permute-done | bytes 1228832 | tf_op jit(solution)/shard_map/ppermute | solution.py:328
  123.6 14.7 %collective-permute-done.10.b_ref = bf16[384,1536]{1,0:T(8,128)(2,1)S(1)} collective-permute-done((bf16[384,1536]{1,0:T(8,128)(2,1)S(1)}, bf16[384,1536]{1,0:T(8,128)(2,1)S(1)}, u32[]{:S(2)}, u32[]{:S(2)}) %collective-permute-start.10) | collective-permute-done | bytes 1179680 | tf_op jit(solution)/shard_map/ppermute | solution.py:328
  138.3 1.0 choose.1
  (26 shorter events, 2.3 us)
Async XLA Ops:
  0.0 3.1 %collective-permute-start.1 = (bf16[384,1536]{1,0:T(8,128)(2,1)}, bf16[384,1536]{1,0:T(8,128)(2,1)S(1)}, u32[]{:S(2)}, u32[]{:S(2)}) collective-permute-start(bf16[384,1536]{1,0:T(8,128)(2,1)} %bitcast.16), channel_id=1, source_target_pairs={{0,1},{1,0},{2,3},{3,2},{4,5},{5,4},{6,7},{7,6},{8,9},{9,8},{10,11... | collective-permute-start | bytes 3538952 | tf_op jit(solution)/shard_map/ppermute | solution.py:328
  0.0 28.6 %collective-permute-start = (bf16[384,1536]{1,0:T(8,128)(2,1)}, bf16[384,1536]{1,0:T(8,128)(2,1)S(1)}, u32[]{:S(2)}, u32[]{:S(2)}) collective-permute-start(bf16[384,1536]{1,0:T(8,128)(2,1)} %bitcast.17), channel_id=1, source_target_pairs={{1,2},{2,1},{3,4},{4,3},{5,6},{6,5},{7,8},{8,7},{9,10},{10,9},{11,... | collective-permute-start | bytes 3538952 | tf_op jit(solution)/shard_map/ppermute | solution.py:330
  3.1 5.0 %copy-start = (bf16[1,1536,4608]{2,1,0:T(8,128)(2,1)S(1)}, bf16[1,1536,4608]{2,1,0:T(8,128)(2,1)}, u32[]{:S(2)}) copy-start(bf16[1,1536,4608]{2,1,0:T(8,128)(2,1)} %param.7) | copy-start | bytes 42467332
  8.1 2.3 %copy-start.2 = (bf16[1,1536,1536]{2,1,0:T(8,128)(2,1)S(1)}, bf16[1,1536,1536]{2,1,0:T(8,128)(2,1)}, u32[]{:S(2)}) copy-start(bf16[1,1536,1536]{2,1,0:T(8,128)(2,1)} %param.8) | copy-start | bytes 14155780
  10.4 1.3 copy-start.4
  11.7 0.7 copy-start.5
  12.4 0.7 copy-start.7
  13.0 15.6 %copy-start.1 = (bf16[1,1536,4608]{2,1,0:T(8,128)(2,1)S(1)}, bf16[1,1536,4608]{2,1,0:T(8,128)(2,1)}, u32[]{:S(2)}) copy-start(bf16[1,1536,4608]{2,1,0:T(8,128)(2,1)} %param.7) | copy-start | bytes 42467332
  13.0 15.6 %copy-start.3 = (bf16[1,1536,1536]{2,1,0:T(8,128)(2,1)S(1)}, bf16[1,1536,1536]{2,1,0:T(8,128)(2,1)}, u32[]{:S(2)}) copy-start(bf16[1,1536,1536]{2,1,0:T(8,128)(2,1)} %param.8) | copy-start | bytes 14155780
  39.5 21.3 %collective-permute-start.3 = (bf16[400,1536]{1,0:T(8,128)(2,1)S(1)}, bf16[400,1536]{1,0:T(8,128)(2,1)S(1)}, u32[]{:S(2)}, u32[]{:S(2)}) collective-permute-start(bf16[400,1536]{1,0:T(8,128)(2,1)S(1)} %far_attention.3), channel_id=1, source_target_pairs={{0,29},{1,18},{2,19},{3,16},{4,17},{5,22},{6,23},{7,20},{8,21},{9,... | collective-permute-start | bytes 3686408 | tf_op jit(solution)/shard_map/ppermute | solution.py:328
  40.8 41.7 %collective-permute-start.6 = (bf16[400,1536]{1,0:T(8,128)(2,1)S(1)}, bf16[400,1536]{1,0:T(8,128)(2,1)S(1)}, u32[]{:S(2)}, u32[]{:S(2)}) collective-permute-start(bf16[400,1536]{1,0:T(8,128)(2,1)S(1)} %far_attention.3), channel_id=1, source_target_pairs={{16,2},{17,13},{18,0},{19,3},{20,6},{21,1},{22,4},{23,7},{24,10},{... | collective-permute-start | bytes 3686408 | tf_op jit(solution)/shard_map/ppermute | solution.py:328
  50.4 44.0 %collective-permute-start.2 = (bf16[400,1536]{1,0:T(8,128)(2,1)S(1)}, bf16[400,1536]{1,0:T(8,128)(2,1)S(1)}, u32[]{:S(2)}, u32[]{:S(2)}) collective-permute-start(bf16[400,1536]{1,0:T(8,128)(2,1)S(1)} %far_attention.3), channel_id=1, source_target_pairs={{16,45},{17,34},{18,35},{19,32},{20,33},{21,38},{22,39},{23,36},{2... | collective-permute-start | bytes 3686408 | tf_op jit(solution)/shard_map/ppermute | solution.py:328
  60.9 5.2 %copy-start.6 = (f32[1,1536]{1,0:T(1,128)S(1)}, f32[1,1536]{1,0:T(1,128)}, u32[]{:S(2)}) copy-start(f32[1,1536]{1,0:T(1,128)} %refs_1_.11) | copy-start | bytes 18436
  60.9 5.2 %copy-start.8 = (s32[1,3]{1,0:T(1,128)S(1)}, s32[1,3]{1,0:T(1,128)}, u32[]{:S(2)}) copy-start(s32[1,3]{1,0:T(1,128)} %lists_ref.11) | copy-start | bytes 40
  60.9 5.2 %collective-permute-start.5 = (bf16[384,1536]{1,0:T(8,128)(2,1)S(1)}, bf16[384,1536]{1,0:T(8,128)(2,1)S(1)}, u32[]{:S(2)}, u32[]{:S(2)}) collective-permute-start(bf16[384,1536]{1,0:T(8,128)(2,1)S(1)} %slice.10), channel_id=1, source_target_pairs={{16,17},{17,16},{18,19},{19,18},{20,21},{21,20},{22,23},{23,22},{2... | collective-permute-start | bytes 3538952 | tf_op jit(solution)/shard_map/ppermute | solution.py:328
  63.7 19.5 %collective-permute-start.4 = (bf16[384,1536]{1,0:T(8,128)(2,1)S(1)}, bf16[384,1536]{1,0:T(8,128)(2,1)S(1)}, u32[]{:S(2)}, u32[]{:S(2)}) collective-permute-start(bf16[384,1536]{1,0:T(8,128)(2,1)S(1)} %slice.9), channel_id=1, source_target_pairs={{0,18},{1,29},{2,16},{3,19},{4,22},{5,17},{6,20},{7,23},{8,26},{9,... | collective-permute-start | bytes 3538952 | tf_op jit(solution)/shard_map/ppermute | solution.py:328
  82.5 14.9 %collective-permute-start.8 = (bf16[400,1536]{1,0:T(8,128)(2,1)S(1)}, bf16[400,1536]{1,0:T(8,128)(2,1)S(1)}, u32[]{:S(2)}, u32[]{:S(2)}) collective-permute-start(bf16[400,1536]{1,0:T(8,128)(2,1)S(1)} %collective-permute-done.6), channel_id=1, source_target_pairs={{0,32},{1,33},{2,34},{3,35},{4,36},{5,37},{6,38},{7,39},{8,40},{9,... | collective-permute-start | bytes 3686408 | tf_op jit(solution)/shard_map/ppermute | solution.py:328
  94.5 2.1 %collective-permute-start.9 = (bf16[384,1536]{1,0:T(8,128)(2,1)S(1)}, bf16[384,1536]{1,0:T(8,128)(2,1)S(1)}, u32[]{:S(2)}, u32[]{:S(2)}) collective-permute-start(bf16[384,1536]{1,0:T(8,128)(2,1)S(1)} %slice.11), channel_id=1, source_target_pairs={{0,1},{1,0},{2,3},{3,2},{4,5},{5,4},{6,7},{7,6},{8,9},{9,8},{10,11... | collective-permute-start | bytes 3538952 | tf_op jit(solution)/shard_map/ppermute | solution.py:328
  95.2 28.4 %collective-permute-start.7 = (bf16[400,1536]{1,0:T(8,128)(2,1)S(1)}, bf16[400,1536]{1,0:T(8,128)(2,1)S(1)}, u32[]{:S(2)}, u32[]{:S(2)}) collective-permute-start(bf16[400,1536]{1,0:T(8,128)(2,1)S(1)} %far_attention.4), channel_id=1, source_target_pairs={{29,32},{18,33},{19,34},{16,35},{17,36},{22,37},{23,38},{20,39},{2... | collective-permute-start | bytes 3686408 | tf_op jit(solution)/shard_map/ppermute | solution.py:328
  98.2 40.1 %collective-permute-start.10 = (bf16[384,1536]{1,0:T(8,128)(2,1)S(1)}, bf16[384,1536]{1,0:T(8,128)(2,1)S(1)}, u32[]{:S(2)}, u32[]{:S(2)}) collective-permute-start(bf16[384,1536]{1,0:T(8,128)(2,1)S(1)} %far_attention.5), channel_id=1, source_target_pairs={{13,16},{2,17},{3,18},{0,19},{1,20},{6,21},{7,22},{4,23},{5,24},{1... | collective-permute-start | bytes 3538952 | tf_op jit(solution)/shard_map/ppermute | solution.py:328

commit v4 on v3

--- a/solution.py
+++ b/solution.py
@@ -14,6 +14,7 @@
 TS = 384
 NBR = 3
 HALF = TS // 2
+SHORT, LOOP, STRAIGHT = range(3)
 THIRD = TS // 3
 WIDE = 768
 N_TILE = 16
@@ -114,9 +115,10 @@
             o_ref[:, pl.ds(first, HD)] = mixed[:, :HD] / total
             lse_ref[...] = jnp.where(lane == 2 * j + i, m + jnp.log2(total), lse_ref[...])
 
-        project_q(0)
-        project_k(0, 0)
-        project_v(0, 0)
+        def project(j, slot):
+            project_q(j)
+            project_k(j, slot)
+            project_v(j, slot)
 
         def step(j, more):
             slot = j % 2
@@ -134,13 +136,23 @@
                 project_v(j + 1, 1 - slot)
             collect(p1, m1, v, j, 1)
 
-        steps(step, False)
+        steps(project, step, {None: SHORT, 1: SHORT, 0: LOOP}[turn])
 
     guarded(run, turn)
 
 
-def steps(step, straight):
-    if straight:
+def steps(project, step, form):
+    if form == SHORT:
+
+        def both(j, carry):
+            project(j, j % 2)
+            step(j, False)
+            return carry
+
+        lax.fori_loop(0, PAIRS, both, 0)
+        return
+    project(0, 0)
+    if form == STRAIGHT:
         for j in range(PAIRS - 1):
             step(j, True)
     else:
@@ -191,8 +203,9 @@
             o = (o_ref[:, pl.ds(first, HD)] * w0 + both[:, :HD] * w1) / (w0 + both[:, HD:] * w1)
             mixed[:, pl.ds(first, HD)] = o.astype(jnp.bfloat16)
 
-        project_k(0, 0)
-        project_v(0, 0)
+        def project(j, slot):
+            project_k(j, slot)
+            project_v(j, slot)
 
         def step(j, more):
             slot = j % 2
@@ -208,7 +221,7 @@
                 project_v(j + 1, 1 - slot)
             collect(p1, m1, v, j, 1)
 
-        steps(step, turn == 0)
+        steps(project, step, {None: STRAIGHT, 1: SHORT, 0: STRAIGHT}[turn])
 
         def finish(j, carry):
             cut = pl.ds(pl.multiple_of(j * WIDE, WIDE), WIDE)

time: 140 us -> 140 us (level)
  Pallas kernels: 56.6 us -> 60.4 us
  waiting for transfers between devices: 47.2 us -> 43.8 us
    ppermute x10, waiting for transfers between devices: 47.2 us -> 43.8 us  [send(): return [lax.ppermute(block, BOTH, perm) for block in blocks]]
    pallas_call x3, Pallas kernels: 32.7 us -> 35.7 us  [near_attention(): pl.pallas_call(functools.partial(near_kernel, turn, len(near)), out_shape...]
  transfers between devices with their start and end apart: 11 -> 11, of which waited for: 5 -> 5; matrix products, arithmetic and copies ran while one was open for 0% -> 0% of each run, Pallas kernels for 32% -> 35%
where the time goes in v4:
time: 140 us; the launch traced here: 139 us
  Pallas kernels  60.4 us (43%)
  waiting for transfers between devices  43.8 us (31%)
  starting transfers between devices  23.5 us (17%)
  local copies, waits for them, and re-layouts  10.2 us (7%)
    ppermute x10, waiting for transfers between devices, send(): return [lax.ppermute(block, BOTH, perm) for block in blocks]  43.8 us
    pallas_call x3, Pallas kernels, near_attention(): pl.pallas_call(functools.partial(near_kernel, turn, len(near)), out_shape...  35.7 us
    pallas_call x3, Pallas kernels, far_attention(): pl.pallas_call(functools.partial(far_kernel, turn, len(far)), out_shape=j...  23.7 us
    ppermute x10, starting transfers between devices, send(): return [lax.ppermute(block, BOTH, perm) for block in blocks]  22.8 us
    unnamed x18, local copies, waits for them, and re-layouts  10 us
  transfers between devices with their start and end apart: 11, of which 5 were waited for; matrix products, arithmetic and copies ran while one was open for 0% of the time, Pallas kernels for 35%

profile of v4, /device:TPU:8, one launch (start us, length us, event | category | flops | bytes accessed | tf_op | source)
XLA Modules:
  0.0 139.0 jit_solution(18312064791139664235)
XLA Ops:
  0.0 0.7 collective-permute-start
  1.4 1.7 %collective-permute-done.1.refs_0_ = bf16[384,1536]{1,0:T(8,128)(2,1)S(1)} collective-permute-done((bf16[384,1536]{1,0:T(8,128)(2,1)}, bf16[384,1536]{1,0:T(8,128)(2,1)S(1)}, u32[]{:S(2)}, u32[]{:S(2)}) %collective-permute-start.1) | collective-permute-done | bytes 1179680 | tf_op jit(solution)/shard_map/ppermute | solution.py:341
  3.1 5.0 %copy-done = bf16[1,1536,4608]{2,1,0:T(8,128)(2,1)S(1)} copy-done((bf16[1,1536,4608]{2,1,0:T(8,128)(2,1)S(1)}, bf16[1,1536,4608]{2,1,0:T(8,128)(2,1)}, u32[]{:S(2)}) %copy-start) | copy-done | bytes 14155800
  8.1 2.3 %copy-done.2 = bf16[1,1536,1536]{2,1,0:T(8,128)(2,1)S(1)} copy-done((bf16[1,1536,1536]{2,1,0:T(8,128)(2,1)S(1)}, bf16[1,1536,1536]{2,1,0:T(8,128)(2,1)}, u32[]{:S(2)}) %copy-start.2) | copy-done | bytes 4718616
  10.4 1.3 copy-done.4
  13.0 16.7 %near_attention.3 = (bf16[384,1536]{1,0:T(8,128)(2,1)S(1)}, f32[384,1536]{1,0:T(8,128)S(1)}, f32[384,128]{1,0:T(8,128)S(1)}) custom-call(s32[1,3]{1,0:T(1,128)S(1)} %copy-done.7, s32[1]{0:T(128)S(6)} %copy.7.counts_ref, bf16[384,1536]{1,0:T(8,128)(2,1)S(1)} %bitcast.18, bf16[384,1536]{1,0:T(8,128)(2,1)S(1)} %collective-permute-done.1.refs_0_, ...), custom_call_target="tpu_custom_call" | custom-call | tf_op jit(solution)/shard_map/near_attention/pallas_call | solution.py:243
  29.8 10.5 %far_attention.3 = bf16[400,1536]{1,0:T(8,128)(2,1)S(1)} custom-call(s32[1,3]{1,0:T(1,128)S(1)} %copy-done.7, s32[1]{0:T(128)S(6)} %copy.7.counts_ref, bf16[384,1536]{1,0:T(8,128)(2,1)S(1)} %bitcast.19, bf16[384,1536]{1,0:T(8,128)(2,1)S(1)} %collective-permute-done.refs_0_, f32[1,1536]{1,0:T(1,128)S(1)} %copy-done.5, ...), custom_call_target="tpu_custom_call" | custom-call | tf_op jit(solution)/shard_map/far_attention/pallas_call | solution.py:264
  40.3 1.3 collective-permute-start.3
  41.6 8.4 %collective-permute-start.6 = (bf16[400,1536]{1,0:T(8,128)(2,1)S(1)}, bf16[400,1536]{1,0:T(8,128)(2,1)S(1)}, u32[]{:S(2)}, u32[]{:S(2)}) collective-permute-start(bf16[400,1536]{1,0:T(8,128)(2,1)S(1)} %far_attention.3), channel_id=1, source_target_pairs={{16,2},{17,13},{18,0},{19,3},{20,6},{21,1},{22,4},{23,7},{24,10},{... | collective-permute-start | bytes 3686408 | tf_op jit(solution)/shard_map/ppermute | solution.py:341
  50.0 5.0 %collective-permute-start.2 = (bf16[400,1536]{1,0:T(8,128)(2,1)S(1)}, bf16[400,1536]{1,0:T(8,128)(2,1)S(1)}, u32[]{:S(2)}, u32[]{:S(2)}) collective-permute-start(bf16[400,1536]{1,0:T(8,128)(2,1)S(1)} %far_attention.3), channel_id=1, source_target_pairs={{16,45},{17,34},{18,35},{19,32},{20,33},{21,38},{22,39},{23,36},{2... | collective-permute-start | bytes 3686408 | tf_op jit(solution)/shard_map/ppermute | solution.py:341
  55.0 5.4 %collective-permute-done.3.own_ref = bf16[400,1536]{1,0:T(8,128)(2,1)S(1)} collective-permute-done((bf16[400,1536]{1,0:T(8,128)(2,1)S(1)}, bf16[400,1536]{1,0:T(8,128)(2,1)S(1)}, u32[]{:S(2)}, u32[]{:S(2)}) %collective-permute-start.3) | collective-permute-done | bytes 1228832 | tf_op jit(solution)/shard_map/ppermute | solution.py:341
  60.5 2.7 %collective-permute-start.5 = (bf16[384,1536]{1,0:T(8,128)(2,1)S(1)}, bf16[384,1536]{1,0:T(8,128)(2,1)S(1)}, u32[]{:S(2)}, u32[]{:S(2)}) collective-permute-start(bf16[384,1536]{1,0:T(8,128)(2,1)S(1)} %slice.10), channel_id=1, source_target_pairs={{16,17},{17,16},{18,19},{19,18},{20,21},{21,20},{22,23},{23,22},{2... | collective-permute-start | bytes 3538952 | tf_op jit(solution)/shard_map/ppermute | solution.py:341
  63.3 1.3 collective-permute-start.4
  64.6 1.1 collective-permute-done.5.refs_0_
  65.7 18.4 %near_attention.4 = (bf16[384,1536]{1,0:T(8,128)(2,1)S(1)}, f32[384,1536]{1,0:T(8,128)S(1)}, f32[384,128]{1,0:T(8,128)S(1)}) custom-call(s32[1,3]{1,0:T(1,128)S(1)} %copy-done.8, s32[1]{0:T(128)S(6)} %copy.7.counts_ref, bf16[400,1536]{1,0:T(8,128)(2,1)S(1)} %collective-permute-done.3.own_ref, bf16[384,1536]{1,0:T(8,128)(2,1)S(1)} %collective-permute-done.5.refs_0_, ...), custom_call_target="tpu_custom_call" | custom-call | tf_op jit(solution)/shard_map/near_attention/pallas_call | solution.py:243
  84.1 0.7 collective-permute-start.8
  84.9 12.4 %far_attention.4 = bf16[400,1536]{1,0:T(8,128)(2,1)S(1)} custom-call(s32[1,3]{1,0:T(1,128)S(1)} %copy-done.8, s32[1]{0:T(128)S(6)} %copy.7.counts_ref, bf16[400,1536]{1,0:T(8,128)(2,1)S(1)} %collective-permute-done.3.own_ref, bf16[384,1536]{1,0:T(8,128)(2,1)S(1)} %collective-permute-done.4.refs_0_, f32[1,1536]{1,0:T(1,128)S(1)} %copy-done.6, ...), custom_call_target="tpu_custom_call" | custom-call | tf_op jit(solution)/shard_map/far_attention/pallas_call | solution.py:264
  97.4 0.7 collective-permute-start.9
  98.1 1.4 collective-permute-start.7
  100.1 0.8 far_attention.5
  100.9 1.3 collective-permute-start.10
  102.2 24.3 %collective-permute-done.7.a_ref = bf16[400,1536]{1,0:T(8,128)(2,1)S(1)} collective-permute-done((bf16[400,1536]{1,0:T(8,128)(2,1)S(1)}, bf16[400,1536]{1,0:T(8,128)(2,1)S(1)}, u32[]{:S(2)}, u32[]{:S(2)}) %collective-permute-start.7) | collective-permute-done | bytes 1228832 | tf_op jit(solution)/shard_map/ppermute | solution.py:341
  126.5 11.4 %collective-permute-done.10.b_ref = bf16[384,1536]{1,0:T(8,128)(2,1)S(1)} collective-permute-done((bf16[384,1536]{1,0:T(8,128)(2,1)S(1)}, bf16[384,1536]{1,0:T(8,128)(2,1)S(1)}, u32[]{:S(2)}, u32[]{:S(2)}) %collective-permute-start.10) | collective-permute-done | bytes 1179680 | tf_op jit(solution)/shard_map/ppermute | solution.py:341
  137.8 1.0 choose.1
  (26 shorter events, 2.2 us)
Async XLA Ops:
  0.0 3.1 %collective-permute-start.1 = (bf16[384,1536]{1,0:T(8,128)(2,1)}, bf16[384,1536]{1,0:T(8,128)(2,1)S(1)}, u32[]{:S(2)}, u32[]{:S(2)}) collective-permute-start(bf16[384,1536]{1,0:T(8,128)(2,1)} %bitcast.16), channel_id=1, source_target_pairs={{0,1},{1,0},{2,3},{3,2},{4,5},{5,4},{6,7},{7,6},{8,9},{9,8},{10,11... | collective-permute-start | bytes 3538952 | tf_op jit(solution)/shard_map/ppermute | solution.py:341
  0.0 29.8 %collective-permute-start = (bf16[384,1536]{1,0:T(8,128)(2,1)}, bf16[384,1536]{1,0:T(8,128)(2,1)S(1)}, u32[]{:S(2)}, u32[]{:S(2)}) collective-permute-start(bf16[384,1536]{1,0:T(8,128)(2,1)} %bitcast.17), channel_id=1, source_target_pairs={{1,2},{2,1},{3,4},{4,3},{5,6},{6,5},{7,8},{8,7},{9,10},{10,9},{11,... | collective-permute-start | bytes 3538952 | tf_op jit(solution)/shard_map/ppermute | solution.py:343
  3.1 5.0 %copy-start = (bf16[1,1536,4608]{2,1,0:T(8,128)(2,1)S(1)}, bf16[1,1536,4608]{2,1,0:T(8,128)(2,1)}, u32[]{:S(2)}) copy-start(bf16[1,1536,4608]{2,1,0:T(8,128)(2,1)} %param.7) | copy-start | bytes 42467332
  8.1 2.3 %copy-start.2 = (bf16[1,1536,1536]{2,1,0:T(8,128)(2,1)S(1)}, bf16[1,1536,1536]{2,1,0:T(8,128)(2,1)}, u32[]{:S(2)}) copy-start(bf16[1,1536,1536]{2,1,0:T(8,128)(2,1)} %param.8) | copy-start | bytes 14155780
  10.4 1.3 copy-start.4
  11.7 0.7 copy-start.5
  12.4 0.7 copy-start.7
  13.0 16.7 %copy-start.1 = (bf16[1,1536,4608]{2,1,0:T(8,128)(2,1)S(1)}, bf16[1,1536,4608]{2,1,0:T(8,128)(2,1)}, u32[]{:S(2)}) copy-start(bf16[1,1536,4608]{2,1,0:T(8,128)(2,1)} %param.7) | copy-start | bytes 42467332
  13.0 16.7 %copy-start.3 = (bf16[1,1536,1536]{2,1,0:T(8,128)(2,1)S(1)}, bf16[1,1536,1536]{2,1,0:T(8,128)(2,1)}, u32[]{:S(2)}) copy-start(bf16[1,1536,1536]{2,1,0:T(8,128)(2,1)} %param.8) | copy-start | bytes 14155780
  40.3 20.1 %collective-permute-start.3 = (bf16[400,1536]{1,0:T(8,128)(2,1)S(1)}, bf16[400,1536]{1,0:T(8,128)(2,1)S(1)}, u32[]{:S(2)}, u32[]{:S(2)}) collective-permute-start(bf16[400,1536]{1,0:T(8,128)(2,1)S(1)} %far_attention.3), channel_id=1, source_target_pairs={{0,29},{1,18},{2,19},{3,16},{4,17},{5,22},{6,23},{7,20},{8,21},{9,... | collective-permute-start | bytes 3686408 | tf_op jit(solution)/shard_map/ppermute | solution.py:341
  41.6 42.6 %collective-permute-start.6 = (bf16[400,1536]{1,0:T(8,128)(2,1)S(1)}, bf16[400,1536]{1,0:T(8,128)(2,1)S(1)}, u32[]{:S(2)}, u32[]{:S(2)}) collective-permute-start(bf16[400,1536]{1,0:T(8,128)(2,1)S(1)} %far_attention.3), channel_id=1, source_target_pairs={{16,2},{17,13},{18,0},{19,3},{20,6},{21,1},{22,4},{23,7},{24,10},{... | collective-permute-start | bytes 3686408 | tf_op jit(solution)/shard_map/ppermute | solution.py:341
  50.0 47.3 %collective-permute-start.2 = (bf16[400,1536]{1,0:T(8,128)(2,1)S(1)}, bf16[400,1536]{1,0:T(8,128)(2,1)S(1)}, u32[]{:S(2)}, u32[]{:S(2)}) collective-permute-start(bf16[400,1536]{1,0:T(8,128)(2,1)S(1)} %far_attention.3), channel_id=1, source_target_pairs={{16,45},{17,34},{18,35},{19,32},{20,33},{21,38},{22,39},{23,36},{2... | collective-permute-start | bytes 3686408 | tf_op jit(solution)/shard_map/ppermute | solution.py:341
  60.5 5.2 %copy-start.6 = (f32[1,1536]{1,0:T(1,128)S(1)}, f32[1,1536]{1,0:T(1,128)}, u32[]{:S(2)}) copy-start(f32[1,1536]{1,0:T(1,128)} %refs_1_.11) | copy-start | bytes 18436
  60.5 5.2 %copy-start.8 = (s32[1,3]{1,0:T(1,128)S(1)}, s32[1,3]{1,0:T(1,128)}, u32[]{:S(2)}) copy-start(s32[1,3]{1,0:T(1,128)} %lists_ref.11) | copy-start | bytes 40
  60.5 5.2 %collective-permute-start.5 = (bf16[384,1536]{1,0:T(8,128)(2,1)S(1)}, bf16[384,1536]{1,0:T(8,128)(2,1)S(1)}, u32[]{:S(2)}, u32[]{:S(2)}) collective-permute-start(bf16[384,1536]{1,0:T(8,128)(2,1)S(1)} %slice.10), channel_id=1, source_target_pairs={{16,17},{17,16},{18,19},{19,18},{20,21},{21,20},{22,23},{23,22},{2... | collective-permute-start | bytes 3538952 | tf_op jit(solution)/shard_map/ppermute | solution.py:341
  63.3 21.6 %collective-permute-start.4 = (bf16[384,1536]{1,0:T(8,128)(2,1)S(1)}, bf16[384,1536]{1,0:T(8,128)(2,1)S(1)}, u32[]{:S(2)}, u32[]{:S(2)}) collective-permute-start(bf16[384,1536]{1,0:T(8,128)(2,1)S(1)} %slice.9), channel_id=1, source_target_pairs={{0,18},{1,29},{2,16},{3,19},{4,22},{5,17},{6,20},{7,23},{8,26},{9,... | collective-permute-start | bytes 3538952 | tf_op jit(solution)/shard_map/ppermute | solution.py:341
  84.1 15.9 %collective-permute-start.8 = (bf16[400,1536]{1,0:T(8,128)(2,1)S(1)}, bf16[400,1536]{1,0:T(8,128)(2,1)S(1)}, u32[]{:S(2)}, u32[]{:S(2)}) collective-permute-start(bf16[400,1536]{1,0:T(8,128)(2,1)S(1)} %collective-permute-done.6), channel_id=1, source_target_pairs={{0,32},{1,33},{2,34},{3,35},{4,36},{5,37},{6,38},{7,39},{8,40},{9,... | collective-permute-start | bytes 3686408 | tf_op jit(solution)/shard_map/ppermute | solution.py:341
  97.4 2.1 %collective-permute-start.9 = (bf16[384,1536]{1,0:T(8,128)(2,1)S(1)}, bf16[384,1536]{1,0:T(8,128)(2,1)S(1)}, u32[]{:S(2)}, u32[]{:S(2)}) collective-permute-start(bf16[384,1536]{1,0:T(8,128)(2,1)S(1)} %slice.11), channel_id=1, source_target_pairs={{0,1},{1,0},{2,3},{3,2},{4,5},{5,4},{6,7},{7,6},{8,9},{9,8},{10,11... | collective-permute-start | bytes 3538952 | tf_op jit(solution)/shard_map/ppermute | solution.py:341
  98.1 28.4 %collective-permute-start.7 = (bf16[400,1536]{1,0:T(8,128)(2,1)S(1)}, bf16[400,1536]{1,0:T(8,128)(2,1)S(1)}, u32[]{:S(2)}, u32[]{:S(2)}) collective-permute-start(bf16[400,1536]{1,0:T(8,128)(2,1)S(1)} %far_attention.4), channel_id=1, source_target_pairs={{29,32},{18,33},{19,34},{16,35},{17,36},{22,37},{23,38},{20,39},{2... | collective-permute-start | bytes 3686408 | tf_op jit(solution)/shard_map/ppermute | solution.py:341
  100.9 37.0 %collective-permute-start.10 = (bf16[384,1536]{1,0:T(8,128)(2,1)S(1)}, bf16[384,1536]{1,0:T(8,128)(2,1)S(1)}, u32[]{:S(2)}, u32[]{:S(2)}) collective-permute-start(bf16[384,1536]{1,0:T(8,128)(2,1)S(1)} %far_attention.5), channel_id=1, source_target_pairs={{13,16},{2,17},{3,18},{0,19},{1,20},{6,21},{7,22},{4,23},{5,24},{1... | collective-permute-start | bytes 3538952 | tf_op jit(solution)/shard_map/ppermute | solution.py:341
